TPU v7x, 128 devices: a whole 4x4x4 slice. The times are simulated.
128 devices in a mesh: inst: 8 (over x_hi, z), dom: 16 (over y, x_lo, core).
Axes of the slice: x: 4 (x_hi: 2, x_lo: 2; x = x_hi * 2 + x_lo), y: 4, z: 4, core: 2. Of those that a mesh axis runs over, the one named last changes fastest.
Arguments:
- flow_state: float32 [8, 6, 4, 1024, 128], P('inst', None, None, 'dom'), may hold values from -0.5 to 3, as said below
- donor_index: int32 [8, 2, 1024], P('inst', None, 'dom'), may hold values from 0 to 1023, as said below
- donor_weight: float32 [8, 2, 1024], P('inst', None, 'dom'), may hold values from 0 to 1
- span_count: int32 [16], P('dom'), may hold values from 64 to 128
Outputs:
- new_state: float32 [8, 6, 4, 1024, 128], P('inst', None, None, 'dom')
- last_update: float32 [8, 6, 4, 1024, 128], P('inst', None, None, 'dom')
Inputs may be any that keep to these rules, and one draw needn't show every extreme that they name: `flow_state`: row 0 (density) lies in 0.8 to 1.2, rows 1 to 3 (momenta) in -0.5 to 0.5, row 4 (energy) in 2 to 3, row 5 (turbulence variable) in 0 to 0.4. For each instance n there is an offset o_n of 0 to 64 - 3 (the rotor's position at that instance), and for each instance, side and cell t a step e of 0 or 1, with donor_index[n, 0, t] = (t + o_n + e) mod 1024 and donor_index[n, 1, t] = (t - o_n - e - 1) mod 1024; o_n + e reaches 62 for some instance and cell on both sides.
All inputs are finite; a program needn't handle non-finite values.
Results may differ from a plain program's by a relative error of at most 0.0003.
Values sent between devices are 32-bit elements; how exact they have to be, the bound alone decides.
A program may use at most 64 MiB of HBM per device.

v0:
```python
import math

import jax
import jax.numpy as jnp
from jax import lax
from jax.sharding import PartitionSpec as P

ITERS = 2


gamma_less = 0.4
dissip_coef = 0.1
visc_coef = 0.02
smooth_coef = 0.5
pseudo_step = 0.05
frequency = 1.0
spectral_visc = 0.1


def extended(block, sides, width):
    for axis, dim in sides:
        count = lax.axis_size(axis)
        forward = [(i, i + 1) for i in range(count - 1)]
        forward.append((count - 1, 0))
        backward = [(target, source) for source, target in forward]
        low = lax.ppermute(
            lax.slice_in_dim(block, block.shape[dim] - width, None, axis=dim), axis, forward
        )
        high = lax.ppermute(lax.slice_in_dim(block, 0, width, axis=dim), axis, backward)
        block = jnp.concatenate([low, block, high], axis=dim)
    return block


def spectral_coefficients(row_ids, column_ids, instances):
    offset = row_ids - column_ids
    phase_angle = math.pi * offset.astype(jnp.float32) / instances
    parity = jnp.where(offset % 2 == 0, 1.0, -1.0)
    safe_sin = jnp.where(offset == 0, 1.0, jnp.sin(phase_angle))
    return jnp.where(offset == 0, 0.0, 0.5 * frequency * parity * jnp.cos(phase_angle) / safe_sin)


def spectral_operator(instances):
    row_ids = jnp.arange(instances, dtype=jnp.int32)
    derivative = spectral_coefficients(row_ids[:, None], row_ids[None, :], instances)
    return derivative - spectral_visc * jnp.dot(
        derivative, derivative, precision=lax.Precision.HIGHEST
    )


def cell_fluxes(current):
    density = current[0]
    velocity = current[1:4] / density
    turbulence = current[5] / density
    pressure = gamma_less * (current[4] - 0.5 * jnp.sum(current[1:4] * velocity, axis=0))
    fluxes = []
    for direction in range(3):
        speed_dir = velocity[direction]
        flux_rows = current * speed_dir
        flux_rows = flux_rows.at[1 + direction].add(pressure)
        flux_rows = flux_rows.at[4].add(pressure * speed_dir)
        fluxes.append(flux_rows)
    primitive = jnp.concatenate([velocity, turbulence[None]], axis=0)
    return (fluxes, primitive)


def spread_viscous(second_prim):
    zero_row = jnp.zeros_like(second_prim[0:1])
    return jnp.concatenate([zero_row, second_prim[0:3], zero_row, second_prim[3:4]], axis=0)


def axial_after(values, ghost):
    half_axial = values.shape[1] // 2
    return jnp.concatenate(
        [values[:, 1:half_axial], ghost, values[:, half_axial + 1 :], values[:, -1:]], axis=1
    )


def axial_before(values, ghost):
    half_axial = values.shape[1] // 2
    return jnp.concatenate(
        [values[:, :1], values[:, : half_axial - 1], ghost, values[:, half_axial:-1]], axis=1
    )


def span_after(values):
    return jnp.concatenate([values[..., 1:], values[..., -1:]], axis=-1)


def span_before(values):
    return jnp.concatenate([values[..., :1], values[..., :-1]], axis=-1)


def residual_terms(padded, ghost_after, ghost_before):
    fluxes, primitive = cell_fluxes(padded)
    fluxes_after, prim_after = cell_fluxes(ghost_after)
    fluxes_before, prim_before = cell_fluxes(ghost_before)
    center = padded[:, :, 1:-1]
    prim_center = primitive[:, :, 1:-1]
    result = 0.5 * (fluxes[1][:, :, 2:] - fluxes[1][:, :, :-2])
    second_state = padded[:, :, 2:] - 2.0 * center + padded[:, :, :-2]
    second_prim = primitive[:, :, 2:] - 2.0 * prim_center + primitive[:, :, :-2]
    flux_axial = fluxes[0][:, :, 1:-1]
    result = result + 0.5 * (
        axial_after(flux_axial, fluxes_after[0]) - axial_before(flux_axial, fluxes_before[0])
    )
    second_state = (
        second_state
        + axial_after(center, ghost_after)
        - 2.0 * center
        + axial_before(center, ghost_before)
    )
    second_prim = (
        second_prim
        + axial_after(prim_center, prim_after)
        - 2.0 * prim_center
        + axial_before(prim_center, prim_before)
    )
    flux_span = fluxes[2][:, :, 1:-1]
    result = result + 0.5 * (span_after(flux_span) - span_before(flux_span))
    second_state = second_state + span_after(center) - 2.0 * center + span_before(center)
    second_prim = (
        second_prim + span_after(prim_center) - 2.0 * prim_center + span_before(prim_center)
    )
    return result - dissip_coef * second_state - visc_coef * spread_viscous(second_prim)


def interpolate(donor_plane, donor_rows, donor_share):
    cells_total = donor_plane.shape[1]
    near_take = jnp.take(donor_plane, donor_rows, axis=1)
    far_take = jnp.take(donor_plane, (donor_rows + 1) % cells_total, axis=1)
    share = donor_share[None, :, None]
    return (share * near_take + (1.0 - share) * far_take)[:, None]


def smooth_once(base, neighbour):
    padded_rim = extended(neighbour, (("dom", 2),), 1)
    return (base + smooth_coef * (padded_rim[:, :, :-2] + padded_rim[:, :, 2:])) / (
        1.0 + 2.0 * smooth_coef
    )


def local(flow_state, donor_index, donor_weight, span_count):
    instances = lax.axis_size("inst")
    own_instance = lax.axis_index("inst")
    matrix = spectral_operator(instances)
    own_row = lax.dynamic_index_in_dim(matrix, own_instance, 0, keepdims=False)
    current = flow_state[0]
    block_cells = current.shape[2]
    annulus_cells = block_cells * lax.axis_size("dom")
    block_start = lax.axis_index("dom") * block_cells
    half_axial = current.shape[1] // 2
    span_pos = jnp.arange(current.shape[3], dtype=jnp.int32)
    active_mask = (span_pos < span_count[0]).astype(jnp.float32)
    update = jnp.zeros_like(current)
    for sweep_index in range(ITERS):
        source = jnp.einsum(
            "m,mvats->vats",
            own_row,
            lax.all_gather(current[None], "inst", axis=0, tiled=True),
            precision=lax.Precision.HIGHEST,
        )
        padded = extended(current, (("dom", 2),), 1)
        planes = jnp.stack([current[:, half_axial - 1], current[:, half_axial]])
        window = extended(planes, (("dom", 2),), block_cells)
        after_local = (donor_index[0, 0] - block_start + block_cells) % annulus_cells
        before_local = (donor_index[0, 1] - block_start + block_cells) % annulus_cells
        ghost_after = interpolate(window[1], after_local, donor_weight[0, 0])
        ghost_before = interpolate(window[0], before_local, donor_weight[0, 1])
        result = source + residual_terms(padded, ghost_after, ghost_before)
        first_pass = smooth_once(result, result)
        smoothed = smooth_once(result, first_pass)
        update = active_mask * smoothed
        current = current - pseudo_step * update
    return (current[None], update[None])


def solution(mesh):
    placed = (
        P("inst", None, None, "dom", None),
        P("inst", None, "dom"),
        P("inst", None, "dom"),
        P("dom"),
    )
    return jax.shard_map(
        local,
        mesh=mesh,
        in_specs=placed,
        out_specs=(P("inst", None, None, "dom", None), P("inst", None, None, "dom", None)),
        check_vma=False,
    )
```

profile of v0, /device:TPU:0, one launch (start us, length us, event | category | flops | bytes accessed | tf_op | source)
XLA Modules:
  0.0 251.1 jit_solution(15784750273571604114)
XLA Ops:
  7.2 0.7 all-gather.4.cloned.1.call-update
  8.4 0.9 fusion.197
  9.3 0.8 pad_maximum_fusion.22
  10.1 3.5 %collective-permute-start.3 = (f32[2,6,64,128]{3,2,1,0:T(8,128)}, f32[2,6,64,128]{3,2,1,0:T(8,128)}, u32[]{:S(2)}, u32[]{:S(2)}) collective-permute-start(f32[2,6,64,128]{3,2,1,0:T(8,128)} %pad_maximum_fusion.22), channel_id=1, source_target_pairs={{1,0},{2,1},{3,2},{4,3},{5,4},{6,5},{7,6},{8,7},{9,8},{10,9},{11,1... | collective-permute-start | bytes 1179656 | tf_op jit(solution)/shard_map/ppermute | solution.py:29
  13.6 3.9 %collective-permute-start.1 = (f32[6,4,1,128]{3,2,1,0:T(1,128)S(1)}, f32[6,4,1,128]{3,2,1,0:T(1,128)S(1)}, u32[]{:S(2)}, u32[]{:S(2)}) collective-permute-start(f32[6,4,1,128]{3,2,1,0:T(1,128)S(1)} %get-tuple-element.333), channel_id=1, source_target_pairs={{1,0},{2,1},{3,2},{4,3},{5,4},{6,5},{7,6},{8,7},{9,8},{10,9},{11,1... | collective-permute-start | bytes 36872 | tf_op jit(solution)/shard_map/ppermute | solution.py:29
  17.5 0.8 fusion.4
  20.1 1.5 fusion.196
  21.5 1.5 fusion.195
  23.0 1.6 collective-permute-done
  25.2 1.0 fusion.83
  26.3 0.9 fusion.186
  27.3 1.2 fusion.70
  28.4 1.4 fusion.185
  29.9 0.8 fusion.114
  30.7 1.5 fusion.184
  32.3 1.2 pad_maximum_fusion
  33.5 0.9 slice_bitcast_fusion.2
  34.4 1.2 copy.337
  35.6 1.7 gather_fusion.3
  37.3 2.4 gather_fusion.2
  39.8 2.3 copy.330
  42.1 2.4 gather_fusion.1
  44.5 2.4 gather_fusion
  47.0 1.3 fusion.89
  48.3 1.2 fusion.90
  50.2 0.8 copy.457
  52.4 49.5 %all-gather.4.cloned.1.call-done = f32[8,6,4,64,128]{4,3,2,1,0:T(8,128)} async-done(((f32[1,6,4,64,128]{4,3,2,1,0:T(8,128)}), f32[8,6,4,64,128]{4,3,2,1,0:T(8,128)}) %all-gather.4.cloned.1.call-update) | async-done | bytes 6291472 | tf_op jit(solution)/shard_map/all_gather | solution.py:159
  101.9 11.4 %fusion.2 = f32[1,6,4,64,128]{4,0,3,2,1:T(1,128)S(1)} fusion(f32[8,6,4,64,128]{4,3,2,1,0:T(8,128)} %all-gather.4.cloned.1.call-done, f32[8,8]{1,0:T(8,128)} %fusion.4, s32[]{:T(128)S(6)} %select_n.75), kind=kOutput, calls=%fused_computation.10 | convolution fusion | flops 18874368 | bytes 7078404 | tf_op jit(solution)/shard_map/m,mvats->vats/dot_general | solution.py:156
  113.5 3.2 %fusion.8 = f32[6,4,64,128]{3,2,0,1:T(8,128)S(1)} fusion(f32[1,4,64,128]{3,2,0,1:T(8,128)S(1)} %broadcast.438, f32[6,4,64,128]{3,2,0,1:T(8,128)S(1)} %bitcast.244, f32[6,1,64,128]{3,2,0,1:T(8,128)} %get-tuple-element.329, f32[6,1,64,128]{3,2,0,1:T(8,128)S(1)} %bitcast.252, f32[6,1,64,128]{3,2,0,1:T(8,128)} %get-tuple-element.331, ...), kind=kLoop, calls=%fused_computation.65 | loop fusion | flops 8060928 | bytes 13262848 | tf_op jit(solution)/shard_map/add | solution.py:169
  116.8 3.8 %collective-permute-start.5 = (f32[6,4,1,128]{3,2,0,1:T(1,128)S(1)}, f32[6,4,1,128]{3,2,0,1:T(1,128)S(1)}, u32[]{:S(2)}, u32[]{:S(2)}) collective-permute-start(f32[6,4,1,128]{3,2,0,1:T(1,128)S(1)} %get-tuple-element.322), channel_id=1, source_target_pairs={{1,0},{2,1},{3,2},{4,3},{5,4},{6,5},{7,6},{8,7},{9,8},{10,9},{11,1... | collective-permute-start | bytes 36872 | tf_op jit(solution)/shard_map/ppermute | solution.py:29
  121.3 0.7 collective-permute-done.4
  122.4 3.9 %collective-permute-start.7 = (f32[6,4,1,128]{3,2,0,1:T(1,128)S(1)}, f32[6,4,1,128]{3,2,0,1:T(1,128)S(1)}, u32[]{:S(2)}, u32[]{:S(2)}) collective-permute-start(f32[6,4,1,128]{3,2,0,1:T(1,128)S(1)} %get-tuple-element.320), channel_id=1, source_target_pairs={{1,0},{2,1},{3,2},{4,3},{5,4},{6,5},{7,6},{8,7},{9,8},{10,9},{11,1... | collective-permute-start | bytes 36872 | tf_op jit(solution)/shard_map/ppermute | solution.py:29
  126.3 1.3 collective-permute-done.6
  128.1 1.0 copy.349
  129.0 0.9 fusion.191
  130.0 3.9 %collective-permute-start.11 = (f32[2,6,64,128]{3,2,1,0:T(8,128)S(1)}, f32[2,6,64,128]{3,2,1,0:T(8,128)S(1)}, u32[]{:S(2)}, u32[]{:S(2)}) collective-permute-start(f32[2,6,64,128]{3,2,1,0:T(8,128)S(1)} %pad_maximum_fusion.23), channel_id=1, source_target_pairs={{1,0},{2,1},{3,2},{4,3},{5,4},{6,5},{7,6},{8,7},{9,8},{10,9},{11,1... | collective-permute-start | bytes 1179656 | tf_op jit(solution)/shard_map/ppermute | solution.py:29
  133.9 3.9 %collective-permute-start.9 = (f32[6,4,1,128]{3,2,1,0:T(1,128)S(1)}, f32[6,4,1,128]{3,2,1,0:T(1,128)S(1)}, u32[]{:S(2)}, u32[]{:S(2)}) collective-permute-start(f32[6,4,1,128]{3,2,1,0:T(1,128)S(1)} %get-tuple-element.317), channel_id=1, source_target_pairs={{1,0},{2,1},{3,2},{4,3},{5,4},{6,5},{7,6},{8,7},{9,8},{10,9},{11,1... | collective-permute-start | bytes 36872 | tf_op jit(solution)/shard_map/ppermute | solution.py:29
  137.9 1.4 fusion.190
  139.3 1.5 fusion.189
  140.8 2.3 collective-permute-done.9
  143.1 2.4 collective-permute-done.8
  146.3 1.0 fusion.68
  147.3 1.2 fusion.55
  148.5 0.9 fusion.181
  149.4 1.5 fusion.183
  151.0 0.8 fusion.110
  151.8 1.4 fusion.182
  153.4 1.2 copy.362
  154.6 1.7 gather_fusion.7
  156.4 2.5 gather_fusion.6
  158.9 1.2 copy.357
  160.1 1.7 gather_fusion.5
  161.8 1.7 gather_fusion.4
  163.7 1.3 fusion.87
  166.0 0.7 copy-done.24
  166.8 49.5 %all-gather.6.cloned.1.call-done = f32[48,4,64,128]{3,2,1,0:T(8,128)} async-done(((f32[6,4,64,128]{3,2,1,0:T(8,128)}), f32[48,4,64,128]{3,2,1,0:T(8,128)}) %all-gather.6.cloned.1.call-update) | async-done | bytes 6291472 | tf_op jit(solution)/shard_map/all_gather | solution.py:159
  216.4 11.4 %fusion = f32[1,6,4,64,128]{4,0,3,2,1:T(1,128)S(1)} fusion(f32[8,6,4,64,128]{4,3,2,1,0:T(8,128)} %bitcast.248, f32[8,8]{1,0:T(8,128)} %fusion.4, s32[]{:T(128)S(6)} %select_n.75), kind=kOutput, calls=%fused_computation.8 | convolution fusion | flops 18874368 | bytes 7078404 | tf_op jit(solution)/shard_map/m,mvats->vats/dot_general | solution.py:156
  227.9 3.1 %fusion.12 = f32[6,4,64,128]{3,2,0,1:T(8,128)S(1)} fusion(f32[1,4,64,128]{3,2,0,1:T(8,128)S(1)} %copy-done.26, f32[6,4,64,128]{3,2,0,1:T(8,128)S(1)} %fusion.36, f32[6,4,64,1]{3,2,0,1:T(8,128)S(1)} %copy-done.12, f32[6,4,64,127]{3,2,0,1:T(8,128)S(1)} %copy-done.10, f32[6,4,64,127]{3,2,0,1:T(8,128)S(1)} %copy-done.9, f32[6,4,64,1]{3,2,0,1:T(8,128)S(1)} %copy-done.11, ...), kind=kLoop, calls=%fused_computation.69 | loop fusion | flops 8060928 | bytes 13262848 | tf_op jit(solution)/shard_map/add | solution.py:169
  231.2 3.8 %collective-permute-start.13 = (f32[6,4,1,128]{3,2,0,1:T(1,128)S(1)}, f32[6,4,1,128]{3,2,0,1:T(1,128)S(1)}, u32[]{:S(2)}, u32[]{:S(2)}) collective-permute-start(f32[6,4,1,128]{3,2,0,1:T(1,128)S(1)} %get-tuple-element.306), channel_id=1, source_target_pairs={{1,0},{2,1},{3,2},{4,3},{5,4},{6,5},{7,6},{8,7},{9,8},{10,9},{11,1... | collective-permute-start | bytes 36872 | tf_op jit(solution)/shard_map/ppermute | solution.py:29
  235.0 1.4 collective-permute-done.12
  236.8 3.9 %collective-permute-start.15 = (f32[6,4,1,128]{3,2,0,1:T(1,128)S(1)}, f32[6,4,1,128]{3,2,0,1:T(1,128)S(1)}, u32[]{:S(2)}, u32[]{:S(2)}) collective-permute-start(f32[6,4,1,128]{3,2,0,1:T(1,128)S(1)} %get-tuple-element.304), channel_id=1, source_target_pairs={{1,0},{2,1},{3,2},{4,3},{5,4},{6,5},{7,6},{8,7},{9,8},{10,9},{11,1... | collective-permute-start | bytes 36872 | tf_op jit(solution)/shard_map/ppermute | solution.py:29
  240.6 1.3 collective-permute-done.14
  242.3 0.9 copy.378
  243.3 0.9 copy.377
  (204 shorter events, 8.8 us)
Async XLA Ops:
  7.2 94.7 %all-gather.4.cloned.1.call-start = ((), (), s32[]{:S(2)}) async-start(), calls=%async_computation | async-start | bytes 7077888 | tf_op jit(solution)/shard_map/all_gather | solution.py:159
  7.9 208.4 %all-gather.6.cloned.1.call-start = ((), (), s32[]{:S(2)}) async-start(), calls=%async_computation.1 | async-start | bytes 7077888 | tf_op jit(solution)/shard_map/all_gather | solution.py:159
  8.4 9.9 %copy-start.49 = (s32[1,2,64]{2,1,0:T(2,128)S(1)}, s32[1,2,64]{2,1,0:T(2,128)}, u32[]{:S(2)}) copy-start(s32[1,2,64]{2,1,0:T(2,128)} %param.47) | copy-start | bytes 1540
  8.4 10.5 %copy-start.48 = (f32[1,2,64]{2,1,0:T(2,128)S(1)}, f32[1,2,64]{2,1,0:T(2,128)}, u32[]{:S(2)}) copy-start(f32[1,2,64]{2,1,0:T(2,128)} %param.48) | copy-start | bytes 1540
  10.1 22.1 %collective-permute-start.3 = (f32[2,6,64,128]{3,2,1,0:T(8,128)}, f32[2,6,64,128]{3,2,1,0:T(8,128)}, u32[]{:S(2)}, u32[]{:S(2)}) collective-permute-start(f32[2,6,64,128]{3,2,1,0:T(8,128)} %pad_maximum_fusion.22), channel_id=1, source_target_pairs={{1,0},{2,1},{3,2},{4,3},{5,4},{6,5},{7,6},{8,7},{9,8},{10,9},{11,1... | collective-permute-start | bytes 1179656 | tf_op jit(solution)/shard_map/ppermute | solution.py:29
  13.6 18.7 %collective-permute-start.2 = (f32[2,6,64,128]{3,2,1,0:T(8,128)}, f32[2,6,64,128]{3,2,1,0:T(8,128)}, u32[]{:S(2)}, u32[]{:S(2)}) collective-permute-start(f32[2,6,64,128]{3,2,1,0:T(8,128)} %pad_maximum_fusion.22), channel_id=1, source_target_pairs={{0,1},{1,2},{2,3},{3,4},{4,5},{5,6},{6,7},{7,8},{8,9},{9,10},{10,1... | collective-permute-start | bytes 1179656 | tf_op jit(solution)/shard_map/ppermute | solution.py:26
  13.6 9.4 %collective-permute-start.1 = (f32[6,4,1,128]{3,2,1,0:T(1,128)S(1)}, f32[6,4,1,128]{3,2,1,0:T(1,128)S(1)}, u32[]{:S(2)}, u32[]{:S(2)}) collective-permute-start(f32[6,4,1,128]{3,2,1,0:T(1,128)S(1)} %get-tuple-element.333), channel_id=1, source_target_pairs={{1,0},{2,1},{3,2},{4,3},{5,4},{6,5},{7,6},{8,7},{9,8},{10,9},{11,1... | collective-permute-start | bytes 36872 | tf_op jit(solution)/shard_map/ppermute | solution.py:29
  17.5 7.1 %collective-permute-start = (f32[6,4,1,128]{3,2,1,0:T(1,128)S(1)}, f32[6,4,1,128]{3,2,1,0:T(1,128)S(1)}, u32[]{:S(2)}, u32[]{:S(2)}) collective-permute-start(f32[6,4,1,128]{3,2,1,0:T(1,128)S(1)} %get-tuple-element.334), channel_id=1, source_target_pairs={{0,1},{1,2},{2,3},{3,4},{4,5},{5,6},{6,7},{7,8},{8,9},{9,10},{10,1... | collective-permute-start | bytes 36872 | tf_op jit(solution)/shard_map/ppermute | solution.py:26
  46.9 2.7 %copy-start.19 = (f32[4,4,64,1]{3,2,0,1:T(8,128)S(1)}, f32[4,4,64,1]{3,2,0,1:T(8,128)}, u32[]{:S(2)}) copy-start(f32[4,4,64,1]{3,2,0,1:T(8,128)} %get-tuple-element.346) | copy-start | bytes 12292
  46.9 2.7 %copy-start.20 = (f32[4,4,64,1]{3,2,0,1:T(8,128)S(1)}, f32[4,4,64,1]{3,2,0,1:T(8,128)}, u32[]{:S(2)}) copy-start(f32[4,4,64,1]{3,2,0,1:T(8,128)} %get-tuple-element.347) | copy-start | bytes 12292
  46.9 2.7 %copy-start.22 = (f32[4,4,64,127]{3,2,0,1:T(8,128)S(1)}, f32[4,4,64,127]{3,2,0,1:T(8,128)}, u32[]{:S(2)}) copy-start(f32[4,4,64,127]{3,2,0,1:T(8,128)} %fusion.83) | copy-start | bytes 1560580
  46.9 2.7 %copy-start.38 = (f32[4,1,64,128]{3,2,0,1:T(8,128)S(1)}, f32[4,1,64,128]{3,2,0,1:T(8,128)}, u32[]{:S(2)}) copy-start(f32[4,1,64,128]{3,2,0,1:T(8,128)} %get-tuple-element.348) | copy-start | bytes 393220
  46.9 2.7 %copy-start.39 = (f32[4,1,64,128]{3,2,0,1:T(8,128)S(1)}, f32[4,1,64,128]{3,2,0,1:T(8,128)}, u32[]{:S(2)}) copy-start(f32[4,1,64,128]{3,2,0,1:T(8,128)} %get-tuple-element.349) | copy-start | bytes 393220
  46.9 2.7 %copy-start.40 = (f32[4,1,64,128]{3,2,0,1:T(8,128)S(1)}, f32[4,1,64,128]{3,2,0,1:T(8,128)}, u32[]{:S(2)}) copy-start(f32[4,1,64,128]{3,2,0,1:T(8,128)} %get-tuple-element.350) | copy-start | bytes 393220
  47.0 2.7 %copy-start.41 = (f32[4,1,64,128]{3,2,0,1:T(8,128)S(1)}, f32[4,1,64,128]{3,2,0,1:T(8,128)}, u32[]{:S(2)}) copy-start(f32[4,1,64,128]{3,2,0,1:T(8,128)} %get-tuple-element.351) | copy-start | bytes 393220
  52.4 61.0 %slice-start = ((f32[4,4,64,128]{3,2,0,1:T(8,128)}), f32[1,4,64,128]{3,2,0,1:T(8,128)S(1)}, s32[]{:S(2)}) async-start(f32[4,4,64,128]{3,2,0,1:T(8,128)} %copy-done.23), calls=%async_computation.2 | async-start | bytes 262144 | tf_op jit(solution)/shard_map/slice | solution.py:68
  52.4 61.0 %slice-start.1 = ((f32[4,4,64,128]{3,2,0,1:T(8,128)}), f32[3,4,64,128]{3,2,0,1:T(8,128)S(1)}, s32[]{:S(2)}) async-start(f32[4,4,64,128]{3,2,0,1:T(8,128)} %copy-done.23), calls=%async_computation.3 | async-start | bytes 786432 | tf_op jit(solution)/shard_map/slice | solution.py:68
  101.9 11.5 %copy-start.1 = (f32[6,4,64,127]{3,2,0,1:T(8,128)S(1)}, f32[6,4,64,127]{3,2,0,1:T(8,128)}, u32[]{:S(2)}) copy-start(f32[6,4,64,127]{3,2,0,1:T(8,128)} %get-tuple-element.325) | copy-start | bytes 2340868
  101.9 11.5 %copy-start.2 = (f32[6,4,64,127]{3,2,0,1:T(8,128)S(1)}, f32[6,4,64,127]{3,2,0,1:T(8,128)}, u32[]{:S(2)}) copy-start(f32[6,4,64,127]{3,2,0,1:T(8,128)} %get-tuple-element.326) | copy-start | bytes 2340868
  101.9 11.5 %copy-start.3 = (f32[6,4,64,1]{3,2,0,1:T(8,128)S(1)}, f32[6,4,64,1]{3,2,0,1:T(8,128)}, u32[]{:S(2)}) copy-start(f32[6,4,64,1]{3,2,0,1:T(8,128)} %get-tuple-element.323) | copy-start | bytes 18436
  101.9 11.5 %copy-start.4 = (f32[6,4,64,1]{3,2,0,1:T(8,128)S(1)}, f32[6,4,64,1]{3,2,0,1:T(8,128)}, u32[]{:S(2)}) copy-start(f32[6,4,64,1]{3,2,0,1:T(8,128)} %get-tuple-element.324) | copy-start | bytes 18436
  101.9 11.5 %copy-start.13 = (f32[6,4,64,127]{3,2,1,0:T(8,128)S(1)}, f32[6,4,64,127]{3,2,1,0:T(8,128)}, u32[]{:S(2)}) copy-start(f32[6,4,64,127]{3,2,1,0:T(8,128)} %get-tuple-element.290) | copy-start | bytes 2340868
  101.9 11.6 %copy-start.14 = (f32[6,4,64,127]{3,2,1,0:T(8,128)S(1)}, f32[6,4,64,127]{3,2,1,0:T(8,128)}, u32[]{:S(2)}) copy-start(f32[6,4,64,127]{3,2,1,0:T(8,128)} %get-tuple-element.291) | copy-start | bytes 2340868
  101.9 11.6 %copy-start.15 = (f32[6,4,64,1]{3,2,1,0:T(8,128)S(1)}, f32[6,4,64,1]{3,2,1,0:T(8,128)}, u32[]{:S(2)}) copy-start(f32[6,4,64,1]{3,2,1,0:T(8,128)} %get-tuple-element.288) | copy-start | bytes 18436
  101.9 11.6 %copy-start.16 = (f32[6,4,64,1]{3,2,1,0:T(8,128)S(1)}, f32[6,4,64,1]{3,2,1,0:T(8,128)}, u32[]{:S(2)}) copy-start(f32[6,4,64,1]{3,2,1,0:T(8,128)} %get-tuple-element.289) | copy-start | bytes 18436
  101.9 11.6 %copy-start.28 = (f32[6,1,64,128]{3,2,1,0:T(8,128)S(1)}, f32[6,1,64,128]{3,2,1,0:T(8,128)}, u32[]{:S(2)}) copy-start(f32[6,1,64,128]{3,2,1,0:T(8,128)} %copy-done.27) | copy-start | bytes 589828
  101.9 11.6 %copy-start.32 = (f32[6,1,64,128]{3,2,1,0:T(8,128)S(1)}, f32[6,1,64,128]{3,2,1,0:T(8,128)}, u32[]{:S(2)}) copy-start(f32[6,1,64,128]{3,2,1,0:T(8,128)} %get-tuple-element.292) | copy-start | bytes 589828
  113.5 3.2 %copy-start.25 = (f32[1,4,64,128]{3,2,0,1:T(8,128)}, f32[1,4,64,128]{3,2,0,1:T(8,128)S(1)}, u32[]{:S(2)}) copy-start(f32[1,4,64,128]{3,2,0,1:T(8,128)S(1)} %broadcast.438) | copy-start | bytes 393220
  116.7 5.3 %collective-permute-start.4 = (f32[6,4,1,128]{3,2,0,1:T(1,128)S(1)}, f32[6,4,1,128]{3,2,0,1:T(1,128)S(1)}, u32[]{:S(2)}, u32[]{:S(2)}) collective-permute-start(f32[6,4,1,128]{3,2,0,1:T(1,128)S(1)} %get-tuple-element.321), channel_id=1, source_target_pairs={{0,1},{1,2},{2,3},{3,4},{4,5},{5,6},{6,7},{7,8},{8,9},{9,10},{10,1... | collective-permute-start | bytes 36872 | tf_op jit(solution)/shard_map/ppermute | solution.py:26
  116.8 5.2 %collective-permute-start.5 = (f32[6,4,1,128]{3,2,0,1:T(1,128)S(1)}, f32[6,4,1,128]{3,2,0,1:T(1,128)S(1)}, u32[]{:S(2)}, u32[]{:S(2)}) collective-permute-start(f32[6,4,1,128]{3,2,0,1:T(1,128)S(1)} %get-tuple-element.322), channel_id=1, source_target_pairs={{1,0},{2,1},{3,2},{4,3},{5,4},{6,5},{7,6},{8,7},{9,8},{10,9},{11,1... | collective-permute-start | bytes 36872 | tf_op jit(solution)/shard_map/ppermute | solution.py:29
  122.3 5.3 %collective-permute-start.6 = (f32[6,4,1,128]{3,2,0,1:T(1,128)S(1)}, f32[6,4,1,128]{3,2,0,1:T(1,128)S(1)}, u32[]{:S(2)}, u32[]{:S(2)}) collective-permute-start(f32[6,4,1,128]{3,2,0,1:T(1,128)S(1)} %get-tuple-element.319), channel_id=1, source_target_pairs={{0,1},{1,2},{2,3},{3,4},{4,5},{5,6},{6,7},{7,8},{8,9},{9,10},{10,1... | collective-permute-start | bytes 36872 | tf_op jit(solution)/shard_map/ppermute | solution.py:26
  122.4 5.3 %collective-permute-start.7 = (f32[6,4,1,128]{3,2,0,1:T(1,128)S(1)}, f32[6,4,1,128]{3,2,0,1:T(1,128)S(1)}, u32[]{:S(2)}, u32[]{:S(2)}) collective-permute-start(f32[6,4,1,128]{3,2,0,1:T(1,128)S(1)} %get-tuple-element.320), channel_id=1, source_target_pairs={{1,0},{2,1},{3,2},{4,3},{5,4},{6,5},{7,6},{8,7},{9,8},{10,9},{11,1... | collective-permute-start | bytes 36872 | tf_op jit(solution)/shard_map/ppermute | solution.py:29
  130.0 23.2 %collective-permute-start.11 = (f32[2,6,64,128]{3,2,1,0:T(8,128)S(1)}, f32[2,6,64,128]{3,2,1,0:T(8,128)S(1)}, u32[]{:S(2)}, u32[]{:S(2)}) collective-permute-start(f32[2,6,64,128]{3,2,1,0:T(8,128)S(1)} %pad_maximum_fusion.23), channel_id=1, source_target_pairs={{1,0},{2,1},{3,2},{4,3},{5,4},{6,5},{7,6},{8,7},{9,8},{10,9},{11,1... | collective-permute-start | bytes 1179656 | tf_op jit(solution)/shard_map/ppermute | solution.py:29
  133.9 19.3 %collective-permute-start.10 = (f32[2,6,64,128]{3,2,1,0:T(8,128)S(1)}, f32[2,6,64,128]{3,2,1,0:T(8,128)S(1)}, u32[]{:S(2)}, u32[]{:S(2)}) collective-permute-start(f32[2,6,64,128]{3,2,1,0:T(8,128)S(1)} %pad_maximum_fusion.23), channel_id=1, source_target_pairs={{0,1},{1,2},{2,3},{3,4},{4,5},{5,6},{6,7},{7,8},{8,9},{9,10},{10,1... | collective-permute-start | bytes 1179656 | tf_op jit(solution)/shard_map/ppermute | solution.py:26
  133.9 9.1 %collective-permute-start.9 = (f32[6,4,1,128]{3,2,1,0:T(1,128)S(1)}, f32[6,4,1,128]{3,2,1,0:T(1,128)S(1)}, u32[]{:S(2)}, u32[]{:S(2)}) collective-permute-start(f32[6,4,1,128]{3,2,1,0:T(1,128)S(1)} %get-tuple-element.317), channel_id=1, source_target_pairs={{1,0},{2,1},{3,2},{4,3},{5,4},{6,5},{7,6},{8,7},{9,8},{10,9},{11,1... | collective-permute-start | bytes 36872 | tf_op jit(solution)/shard_map/ppermute | solution.py:29
  137.9 7.6 %collective-permute-start.8 = (f32[6,4,1,128]{3,2,1,0:T(1,128)S(1)}, f32[6,4,1,128]{3,2,1,0:T(1,128)S(1)}, u32[]{:S(2)}, u32[]{:S(2)}) collective-permute-start(f32[6,4,1,128]{3,2,1,0:T(1,128)S(1)} %get-tuple-element.318), channel_id=1, source_target_pairs={{0,1},{1,2},{2,3},{3,4},{4,5},{5,6},{6,7},{7,8},{8,9},{9,10},{10,1... | collective-permute-start | bytes 36872 | tf_op jit(solution)/shard_map/ppermute | solution.py:26
  158.8 4.7 %copy-start.43 = (pred[64]{0:T(512)(128)(4,1)S(1)}, pred[64]{0:T(512)(128)(4,1)}, u32[]{:S(2)}) copy-start(pred[64]{0:T(512)(128)(4,1)} %get-tuple-element.267) | copy-start | bytes 196
  158.8 4.8 %copy-start.46 = (f32[64]{0:T(128)S(1)}, f32[64]{0:T(128)}, u32[]{:S(2)}) copy-start(f32[64]{0:T(128)} %get-tuple-element.370) | copy-start | bytes 772
  158.8 4.8 %copy-start.47 = (f32[64]{0:T(128)S(1)}, f32[64]{0:T(128)}, u32[]{:S(2)}) copy-start(f32[64]{0:T(128)} %get-tuple-element.372) | copy-start | bytes 772
  158.8 6.2 %copy-start.42 = (pred[64]{0:T(512)(128)(4,1)S(1)}, pred[64]{0:T(512)(128)(4,1)}, u32[]{:S(2)}) copy-start(pred[64]{0:T(512)(128)(4,1)} %get-tuple-element.378) | copy-start | bytes 196
  158.8 6.2 %copy-start.44 = (f32[64]{0:T(128)S(1)}, f32[64]{0:T(128)}, u32[]{:S(2)}) copy-start(f32[64]{0:T(128)} %get-tuple-element.371) | copy-start | bytes 772
  158.9 6.2 %copy-start.45 = (f32[64]{0:T(128)S(1)}, f32[64]{0:T(128)}, u32[]{:S(2)}) copy-start(f32[64]{0:T(128)} %get-tuple-element.373) | copy-start | bytes 772
  163.6 1.7 copy-start.17
  163.6 1.7 copy-start.18
  163.6 1.7 copy-start.21
  166.7 61.1 %copy-start.29 = (f32[6,1,64,128]{3,2,1,0:T(8,128)S(1)}, f32[6,1,64,128]{3,2,1,0:T(8,128)}, u32[]{:S(2)}) copy-start(f32[6,1,64,128]{3,2,1,0:T(8,128)} %get-tuple-element.279) | copy-start | bytes 589828
  166.7 61.1 %copy-start.30 = (f32[6,1,64,128]{3,2,1,0:T(8,128)S(1)}, f32[6,1,64,128]{3,2,1,0:T(8,128)}, u32[]{:S(2)}) copy-start(f32[6,1,64,128]{3,2,1,0:T(8,128)} %get-tuple-element.280) | copy-start | bytes 589828
  166.7 61.1 %copy-start.31 = (f32[6,1,64,128]{3,2,1,0:T(8,128)S(1)}, f32[6,1,64,128]{3,2,1,0:T(8,128)}, u32[]{:S(2)}) copy-start(f32[6,1,64,128]{3,2,1,0:T(8,128)} %get-tuple-element.281) | copy-start | bytes 589828
  166.8 49.5 %copy-start.33 = (f32[6,1,64,128]{3,2,1,0:T(8,128)}, f32[6,1,64,128]{3,2,1,0:T(8,128)S(1)}, u32[]{:S(2)}) copy-start(f32[6,1,64,128]{3,2,1,0:T(8,128)S(1)} %fusion.119) | copy-start | bytes 589828
  216.3 11.5 %copy-start.5 = (f32[6,4,64,127]{3,2,0,1:T(8,128)S(1)}, f32[6,4,64,127]{3,2,0,1:T(8,128)}, u32[]{:S(2)}) copy-start(f32[6,4,64,127]{3,2,0,1:T(8,128)} %get-tuple-element.309) | copy-start | bytes 2340868
  216.3 11.5 %copy-start.6 = (f32[6,4,64,127]{3,2,0,1:T(8,128)S(1)}, f32[6,4,64,127]{3,2,0,1:T(8,128)}, u32[]{:S(2)}) copy-start(f32[6,4,64,127]{3,2,0,1:T(8,128)} %get-tuple-element.310) | copy-start | bytes 2340868
  216.3 11.6 %copy-start.7 = (f32[6,4,64,1]{3,2,0,1:T(8,128)S(1)}, f32[6,4,64,1]{3,2,0,1:T(8,128)}, u32[]{:S(2)}) copy-start(f32[6,4,64,1]{3,2,0,1:T(8,128)} %get-tuple-element.307) | copy-start | bytes 18436
  216.3 11.6 %copy-start.8 = (f32[6,4,64,1]{3,2,0,1:T(8,128)S(1)}, f32[6,4,64,1]{3,2,0,1:T(8,128)}, u32[]{:S(2)}) copy-start(f32[6,4,64,1]{3,2,0,1:T(8,128)} %get-tuple-element.308) | copy-start | bytes 18436
  216.3 11.6 %copy-start.9 = (f32[6,4,64,127]{3,2,0,1:T(8,128)S(1)}, f32[6,4,64,127]{3,2,0,1:T(8,128)}, u32[]{:S(2)}) copy-start(f32[6,4,64,127]{3,2,0,1:T(8,128)} %get-tuple-element.286) | copy-start | bytes 2340868
  216.3 11.6 %copy-start.10 = (f32[6,4,64,127]{3,2,0,1:T(8,128)S(1)}, f32[6,4,64,127]{3,2,0,1:T(8,128)}, u32[]{:S(2)}) copy-start(f32[6,4,64,127]{3,2,0,1:T(8,128)} %get-tuple-element.287) | copy-start | bytes 2340868
  216.3 11.6 %copy-start.11 = (f32[6,4,64,1]{3,2,0,1:T(8,128)S(1)}, f32[6,4,64,1]{3,2,0,1:T(8,128)}, u32[]{:S(2)}) copy-start(f32[6,4,64,1]{3,2,0,1:T(8,128)} %get-tuple-element.284) | copy-start | bytes 18436
  216.3 11.6 %copy-start.12 = (f32[6,4,64,1]{3,2,0,1:T(8,128)S(1)}, f32[6,4,64,1]{3,2,0,1:T(8,128)}, u32[]{:S(2)}) copy-start(f32[6,4,64,1]{3,2,0,1:T(8,128)} %get-tuple-element.285) | copy-start | bytes 18436
  216.3 11.6 %slice-start.2 = ((f32[4,4,64,128]{3,2,0,1:T(8,128)}), f32[1,4,64,128]{3,2,0,1:T(8,128)S(1)}, s32[]{:S(2)}) async-start(f32[4,4,64,128]{3,2,0,1:T(8,128)} %copy-done.24), calls=%async_computation.4 | async-start | bytes 262144 | tf_op jit(solution)/shard_map/slice | solution.py:68
  216.4 11.6 %slice-start.3 = ((f32[4,4,64,128]{3,2,0,1:T(8,128)}), f32[3,4,64,128]{3,2,0,1:T(8,128)S(1)}, s32[]{:S(2)}) async-start(f32[4,4,64,128]{3,2,0,1:T(8,128)} %copy-done.24), calls=%async_computation.5 | async-start | bytes 786432 | tf_op jit(solution)/shard_map/slice | solution.py:68
  216.4 11.6 %copy-start.26 = (f32[1,4,64,128]{3,2,0,1:T(8,128)S(1)}, f32[1,4,64,128]{3,2,0,1:T(8,128)}, u32[]{:S(2)}) copy-start(f32[1,4,64,128]{3,2,0,1:T(8,128)} %copy-done.25) | copy-start | bytes 393220
  231.1 5.3 %collective-permute-start.12 = (f32[6,4,1,128]{3,2,0,1:T(1,128)S(1)}, f32[6,4,1,128]{3,2,0,1:T(1,128)S(1)}, u32[]{:S(2)}, u32[]{:S(2)}) collective-permute-start(f32[6,4,1,128]{3,2,0,1:T(1,128)S(1)} %get-tuple-element.305), channel_id=1, source_target_pairs={{0,1},{1,2},{2,3},{3,4},{4,5},{5,6},{6,7},{7,8},{8,9},{9,10},{10,1... | collective-permute-start | bytes 36872 | tf_op jit(solution)/shard_map/ppermute | solution.py:26
  231.2 5.2 %collective-permute-start.13 = (f32[6,4,1,128]{3,2,0,1:T(1,128)S(1)}, f32[6,4,1,128]{3,2,0,1:T(1,128)S(1)}, u32[]{:S(2)}, u32[]{:S(2)}) collective-permute-start(f32[6,4,1,128]{3,2,0,1:T(1,128)S(1)} %get-tuple-element.306), channel_id=1, source_target_pairs={{1,0},{2,1},{3,2},{4,3},{5,4},{6,5},{7,6},{8,7},{9,8},{10,9},{11,1... | collective-permute-start | bytes 36872 | tf_op jit(solution)/shard_map/ppermute | solution.py:29
  236.7 5.3 %collective-permute-start.14 = (f32[6,4,1,128]{3,2,0,1:T(1,128)S(1)}, f32[6,4,1,128]{3,2,0,1:T(1,128)S(1)}, u32[]{:S(2)}, u32[]{:S(2)}) collective-permute-start(f32[6,4,1,128]{3,2,0,1:T(1,128)S(1)} %get-tuple-element.303), channel_id=1, source_target_pairs={{0,1},{1,2},{2,3},{3,4},{4,5},{5,6},{6,7},{7,8},{8,9},{9,10},{10,1... | collective-permute-start | bytes 36872 | tf_op jit(solution)/shard_map/ppermute | solution.py:26
  236.8 5.3 %collective-permute-start.15 = (f32[6,4,1,128]{3,2,0,1:T(1,128)S(1)}, f32[6,4,1,128]{3,2,0,1:T(1,128)S(1)}, u32[]{:S(2)}, u32[]{:S(2)}) collective-permute-start(f32[6,4,1,128]{3,2,0,1:T(1,128)S(1)} %get-tuple-element.304), channel_id=1, source_target_pairs={{1,0},{2,1},{3,2},{4,3},{5,4},{6,5},{7,6},{8,7},{9,8},{10,9},{11,1... | collective-permute-start | bytes 36872 | tf_op jit(solution)/shard_map/ppermute | solution.py:29
  (8 other events, 10.2 us)
Sparse Core Ops, SparseCore 0:
  10.3 91.5 all-gather.3
  129.2 87.0 all-gather.5
where the time goes:
time: 252 us; the launch traced here: 251 us
  waiting for transfers between devices  111 us (44%)
  local copies, waits for them, and re-layouts  45.5 us (18%)
  starting transfers between devices  31.1 us (12%)
  other arithmetic  24 us (10%)
  matrix products  23.6 us (9%)
  between operations  15.9 us (6%)
    all_gather x2, waiting for transfers between devices, local(): lax.all_gather(current[None], 'inst', axis=0, tiled=True)  99 us
    ppermute x8, starting transfers between devices, extended(): lax.ppermute(lax.slice_in_dim(block, 0, width, axis=dim), axis, backward)  30.7 us
    dot_general x2, matrix products, local(): jnp.einsum('m,mvats->vats', own_row, lax.all_gather(current[None], 'inst'...  22.8 us
    slice x8, local copies, waits for them, and re-layouts, span_before(): return jnp.concatenate([values[..., :1], values[..., :-1]], axis=-1)  11.8 us
    gather x4, local copies, waits for them, and re-layouts, interpolate(): near_take = jnp.take(donor_plane, donor_rows, axis=1)  9.04 us
    ppermute x8, waiting for transfers between devices, extended(): lax.ppermute(lax.slice_in_dim(block, block.shape[dim] - width, None, axis...  8.73 us
    gather x4, local copies, waits for them, and re-layouts, interpolate(): far_take = jnp.take(donor_plane, (donor_rows + 1) % cells_total, axis=1)  7.61 us
    add x2, other arithmetic, local(): result = source + residual_terms(padded, ghost_after, ghost_before)  6.32 us
  transfers between devices with their start and end apart: 18, of which 11 were waited for; matrix products, arithmetic and copies ran while one was open for 23% of the time, Pallas kernels for 0%

commit v1 on v0

v1 whole, which is shorter than its diff:
```python
import functools
import math

import jax
import jax.numpy as jnp
import numpy as np
from jax import lax
from jax.experimental import pallas as pl
from jax.experimental.pallas import tpu as pltpu
from jax.sharding import PartitionSpec as P

ITERS = 2
NI = 8
NV = 6
AX = 4
PL = NV * AX
PER = PL // NI
T = 64
S = 128
PARTS = ((0, 16), (T - 16, 16), (16, T - 32))
MESH = pl.DeviceIdType.MESH


def spectral_row():
    k = np.arange(NI)[:, None] - np.arange(NI)[None, :]
    safe = np.where(k == 0, 1.0, np.sin(math.pi * k / NI))
    deriv = np.where(k == 0, 0.0, 0.5 * (-1.0) ** k * np.cos(math.pi * k / NI) / safe)
    return (deriv - 0.1 * deriv @ deriv)[:, 0]


def spectral_apply(x):
    row = spectral_row()
    even = [float(row[j] + row[j + 4]) / 2 for j in range(4)]
    odd = [float(row[j] - row[j + 4]) / 2 for j in range(4)]
    s = [x[z] + x[z + 4] for z in range(4)]
    d = [x[z] - x[z + 4] for z in range(4)]
    q0, q1 = s[0] - s[2], s[1] - s[3]
    s0 = even[0] * q0 + even[3] * q1
    s1 = even[1] * q0 + even[0] * q1
    sym = [s0, s1, -s0, -s1]
    out = [None] * NI
    for z in range(4):
        acc = None
        for y in range(4):
            coef = odd[z - y] if y <= z else -odd[4 + z - y]
            term = coef * d[y]
            acc = term if acc is None else acc + term
        out[z] = sym[z] + acc
        out[z + 4] = sym[z] - acc
    return out


def primitives(u):
    inv = 1.0 / u[0]
    vel = [u[1] * inv, u[2] * inv, u[3] * inv]
    nu = u[5] * inv
    pres = 0.4 * (u[4] - 0.5 * (u[1] * vel[0] + u[2] * vel[1] + u[3] * vel[2]))
    return vel, nu, pres


def centre_terms(u, vel, nu):
    return [
        0.1 * u[0],
        0.1 * u[1] + 0.02 * vel[0],
        0.1 * u[2] + 0.02 * vel[1],
        0.1 * u[3] + 0.02 * vel[2],
        0.1 * u[4],
        0.1 * u[5] + 0.02 * nu,
    ]


def half_flux(u, vel, pres, k):
    h = 0.5 * vel[k]
    f = [0.5 * u[1 + k], u[1] * h, u[2] * h, u[3] * h, (u[4] + pres) * h, u[5] * h]
    f[1 + k] = f[1 + k] + 0.5 * pres
    return f


def next_terms(u, k):
    vel, nu, pres = primitives(u)
    c = centre_terms(u, vel, nu)
    return [f - g for f, g in zip(half_flux(u, vel, pres, k), c)]


def prev_terms(u, k):
    vel, nu, pres = primitives(u)
    c = centre_terms(u, vel, nu)
    return [-(f + g) for f, g in zip(half_flux(u, vel, pres, k), c)]


def kernel(
    n_dom,
    n_cells,
    flow,
    idx,
    wgt,
    count,
    new_state,
    last_update,
    idx_s,
    count_s,
    idx_v,
    wgt_v,
    cur,
    in_u,
    in_n,
    w1,
    w2,
    ss,
    ww,
    n0,
    n1,
    rr,
    a2,
    b2,
    coef,
    win,
    edge,
    halo,
    redge,
    rhalo,
    qedge,
    qhalo,
    r2,
    wedge,
    whalo,
    load_sem,
    p_send,
    p_recv,
    d_send,
    d_recv,
):
    inst = lax.axis_index("inst")
    dom = lax.axis_index("dom")
    left = lax.rem(dom + n_dom - 1, n_dom)
    right = lax.rem(dom + 1, n_dom)
    work = dom + 2 - 4 * lax.rem(dom // 2, 2)

    loads = [
        pltpu.make_async_copy(source, target, load_sem.at[n])
        for n, (source, target) in enumerate(
            ((flow, cur), (idx, idx_s), (idx, idx_v), (wgt, wgt_v), (count, count_s))
        )
    ]
    for c in loads:
        c.start()
    barrier = pltpu.get_barrier_semaphore()
    for j in range(NI):
        pl.semaphore_signal(barrier, inc=1, device_id=(j, work), device_id_type=MESH)
    for d in (left, right):
        pl.semaphore_signal(barrier, inc=1, device_id=(inst, d), device_id_type=MESH)

    def cut(unit, part):
        if unit == 3 and part >= 2:
            return PARTS[2] + (part - 2, 1)
        return PARTS[part] + (0, PER)

    def piece(unit, partner, part, slot):
        at, size, k0, kn = cut(unit, part)
        rows = pl.ds(at, size)
        some = pl.ds(k0, kn)
        mine = pl.ds(PER * partner + k0, kn)
        theirs = pl.ds(PER * slot + k0, kn)
        if unit == 0:
            source, target = flow.at[mine, rows], in_u.at[slot, some, rows]
        elif unit == 1:
            source, target = w1.at[partner, some, rows], ss.at[theirs, rows]
        elif unit == 2:
            source, target = n0.at[mine, rows], in_n.at[slot, some, rows]
        else:
            source, target = w2.at[partner, some, rows], ww.at[slot, some, pl.ds(8 + at, size)]
        return pltpu.make_async_remote_copy(
            src_ref=source,
            dst_ref=target,
            send_sem=p_send.at[unit],
            recv_sem=p_recv.at[unit, part],
            device_id=(partner, work),
            device_id_type=MESH,
        )

    order = [lax.rem(inst + n, NI) for n in range(NI)]

    def send(unit, part):
        for j in order:
            piece(unit, j, part, inst).start()

    def arrive(unit, part):
        at, size, k0, kn = cut(unit, part)
        rows = pl.ds(at, size)
        if unit == 3:
            ref = ww.at[:, pl.ds(k0, kn), pl.ds(8 + at, size)]
        else:
            ref = (in_u.at[:, :, rows], ss.at[:, rows], in_n.at[:, :, rows])[unit]
        pltpu.make_async_copy(ref, ref, p_recv.at[unit, part]).wait()

    def gone(unit):
        ref = (flow, w1, n0, w2)[unit]
        pltpu.make_async_copy(ref, ref, p_send.at[unit]).wait()

    def planes(n, group, body):
        def step(i, _):
            for k in range(group):
                body(group * i + k)
            return 0

        lax.fori_loop(0, n // group, step, 0)

    def near(slot, source, target, device):
        return pltpu.make_async_remote_copy(
            src_ref=source,
            dst_ref=target,
            send_sem=d_send.at[slot],
            recv_sem=d_recv.at[slot],
            device_id=(inst, device),
            device_id_type=MESH,
        )

    def both(slot, out, back):
        return [
            near(slot, out.at[0], back.at[1], left),
            near(slot + 1, out.at[1], back.at[0], right),
        ]

    def spectral(part, source, target, extra=None, k0=0, kn=PER):
        at, size = PARTS[part]

        def step(n, _):
            k = k0 + n // (size // 16)
            t0 = pl.multiple_of(at + 16 * lax.rem(n, size // 16), 16)
            x = [source[m, k, pl.ds(t0, 16), :] for m in range(NI)]
            if extra is not None:
                x = [g + extra[m, k, pl.ds(t0, 16), :] for m, g in enumerate(x)]
            got = spectral_apply(x)
            for m in range(NI):
                target[m, k, pl.ds(t0, 16), :] = got[m]
            return 0

        lax.fori_loop(0, kn * size // 16, step, 0)

    lane = lax.broadcasted_iota(jnp.int32, (8, S), 1)
    first_lane = lane == 0
    last_lane = lane == S - 1

    def inside(out, start, stop):
        def tile(i, _):
            t0 = pl.multiple_of(8 * i, 8)
            total = []
            first = []
            second = []
            for a in range(AX):
                u = [cur[v * AX + a, pl.ds(t0, 8), :] for v in range(NV)]
                vel, nu, pres = primitives(u)
                c = centre_terms(u, vel, nu)
                f1 = half_flux(u, vel, pres, 0)
                first.append([f - g for f, g in zip(f1, c)])
                second.append([f + g for f, g in zip(f1, c)])
                f2 = half_flux(u, vel, pres, 1)
                f3 = half_flux(u, vel, pres, 2)
                mine = []
                for v in range(NV):
                    a2[v * AX + a, pl.ds(t0 + 8, 8), :] = f2[v] - c[v]
                    b2[v * AX + a, pl.ds(t0 + 8, 8), :] = f2[v] + c[v]
                    up = f3[v] - c[v]
                    down = f3[v] + c[v]
                    after = jnp.where(last_lane, up, pltpu.roll(up, S - 1, 1))
                    before = jnp.where(first_lane, down, pltpu.roll(down, 1, 1))
                    mine.append(6.0 * c[v] + (after - before))
                total.append(mine)
            for a in range(AX):
                for v in range(NV):
                    r = total[a][v]
                    if a == AX - 1:
                        r = r + first[a][v]
                    elif a != AX // 2 - 1:
                        r = r + first[a + 1][v]
                    if a == 0:
                        r = r - second[a][v]
                    elif a != AX // 2:
                        r = r - second[a - 1][v]
                    out[v * AX + a, pl.ds(t0, 8), :] = r
            return 0

        lax.fori_loop(start, stop, tile, 0)

    def around(out, it, layers, windows, base):
        for c in layers:
            c.wait_recv()
        low = prev_terms([halo[it, 0, AX * v : AX * v + AX, :] for v in range(NV)], 1)
        high = next_terms([halo[it, 1, AX * v : AX * v + AX, :] for v in range(NV)], 1)
        for v in range(NV):
            for a in range(AX):
                b2[v * AX + a, 7:8, :] = -low[v][a : a + 1]
                a2[v * AX + a, T + 8 : T + 9, :] = high[v][a : a + 1]

        def plane(p):
            out[p] += a2[p, 9 : T + 9] - b2[p, 7 : T + 7]

        planes(PL, 3, plane)
        for c in windows:
            c.wait_recv()

        def ghosts(i, _):
            t0 = pl.multiple_of(8 * i, 8)
            for side in range(2):
                taps = [coef[side, n, pl.ds(t0, 8), :] for n in range(3)]
                u = []
                for v in range(NV):
                    g = taps[0] * win[it, side, v, pl.ds(base[side] + t0, 8), :]
                    g = g + taps[1] * win[it, side, v, pl.ds(base[side] + t0 + 1, 8), :]
                    g = g + taps[2] * win[it, side, v, pl.ds(base[side] + t0 + 2, 8), :]
                    u.append(g)
                terms = next_terms(u, 0) if side == 0 else prev_terms(u, 0)
                for v in range(NV):
                    out[v * AX + 1 + side, pl.ds(t0, 8), :] += terms[v]
            return 0

        lax.fori_loop(0, T // 8, ghosts, 0)

    def rims(it):
        edge[it, 0, 0:PL] = cur[:, 0, :]
        edge[it, 1, 0:PL] = cur[:, T - 1, :]
        for side in range(2):
            edge[it, side, PL : PL + 8] = jnp.broadcast_to(active, (8, S))
        for v in range(NV):
            win[it, 0, v, 0:T] = cur[v * AX + 2]
            win[it, 1, v, T : 2 * T] = cur[v * AX + 1]
        layers = both(10 * it, edge.at[it], halo.at[it])
        windows = [
            near(10 * it + 2, win.at[it, 0, :, 0:T], win.at[it, 0, :, T : 2 * T], left),
            near(10 * it + 3, win.at[it, 1, :, T : 2 * T], win.at[it, 1, :, 0:T], right),
        ]
        return layers, windows

    pl.semaphore_wait(barrier, NI + 2)
    send(0, 0)
    send(0, 1)
    for c in loads:
        c.wait()
    active = jnp.where(lax.broadcasted_iota(jnp.int32, (1, S), 1) < count_s[0], 1.0, 0.0)
    layers, windows = rims(0)
    for c in layers + windows:
        c.start()
    send(0, 2)

    def least(t, low):
        cell = dom * T + t
        gaps = (idx_s[0, t] - cell, cell - 1 - idx_s[1, t])
        gaps = [jnp.where(g < 0, g + n_cells, g) for g in gaps]
        return jnp.minimum(low[0], gaps[0]), jnp.minimum(low[1], gaps[1])

    start = (jnp.int32(n_cells), jnp.int32(n_cells))
    offset = [jnp.clip(x, 0, T - 2) for x in lax.fori_loop(0, T, least, start)]
    base = [offset[0], T - 2 - offset[1]]
    eye = lax.broadcasted_iota(jnp.int32, (T, T), 0) == lax.broadcasted_iota(
        jnp.int32, (T, T), 1
    )
    for side in range(2):
        cell = dom * T + lax.broadcasted_iota(jnp.int32, (1, T), 1)
        row = idx_v[side : side + 1, :]
        gap = row - cell if side == 0 else cell - 1 - row
        gap = jnp.where(gap < 0, gap + n_cells, gap)
        step = jnp.where(gap > offset[side], 1.0, 0.0)
        w = wgt_v[side : side + 1, :]
        taps = [(1.0 - step) * w, step * w + (1.0 - step) * (1.0 - w), step * (1.0 - w)]
        if side == 1:
            taps = [step * w, (1.0 - step) * w + step * (1.0 - w), (1.0 - step) * (1.0 - w)]
        for i, tap in enumerate(taps):
            column = jnp.sum(jnp.where(eye, tap, 0.0), axis=1, keepdims=True)
            coef[side, i] = jnp.broadcast_to(column, (T, S))

    half = T // 16
    inside(n0, 0, half)
    for part in (0, 1):
        arrive(0, part)
        spectral(part, in_u, w1)
        send(1, part)
    inside(n0, half, 2 * half)
    arrive(0, 2)
    spectral(2, in_u, w1)
    send(1, 2)
    around(n0, 0, layers, windows, base)
    for part in (0, 1, 2):
        send(2, part)

    arrive(1, 0)
    arrive(1, 1)
    for n, t in enumerate((0, 1, T - 2, T - 1)):
        redge[0, n // 2, n % 2] = n0[:, t, :] + ss[:, t, :]
    rim = both(4, redge.at[0], rhalo.at[0])
    for c in rim:
        c.start()
    arrive(1, 2)

    def add_source(p):
        rr[p, 8 : T + 8] = n0[p] + ss[p]

    planes(PL, 3, add_source)
    for c in rim:
        c.wait()
    for n, t in enumerate((-2, -1, T, T + 1)):
        rr[:, 8 + t, :] = rhalo[0, n // 2, n % 2]
    gone(0)
    for c in layers + windows:
        c.wait_send()

    def smoothed(ref, p):
        return (
            0.625 * ref[p, 8 : T + 8]
            + 0.125 * (ref[p, 7 : T + 7] + ref[p, 9 : T + 9])
            + 0.0625 * (ref[p, 6 : T + 6] + ref[p, 10 : T + 10])
        )

    def first_update(p):
        cur[p] = cur[p] - 0.05 * (smoothed(rr, p) * active)

    planes(PL, 2, first_update)
    layers, windows = rims(1)
    for c in layers + windows:
        c.start()

    for part in (0, 1):
        arrive(2, part)
        spectral(part, in_n, w2, w1)
        send(3, part)
    inside(n1, 0, half)
    arrive(2, 2)
    for k in range(PER):
        spectral(2, in_n, w2, w1, k, 1)
        send(3, 2 + k)
    inside(n1, half, 2 * half)
    around(n1, 1, layers, windows, base)
    for n, t in enumerate((0, 1, T - 2, T - 1)):
        for k in range(PER):
            rows = [n1[PER * j + k, t : t + 1, :] + ss[PER * j + k, t : t + 1, :] for j in range(NI)]
            qedge[n // 2, n % 2, k] = jnp.concatenate(rows, axis=0)
    rim = both(6, qedge, qhalo)
    for c in rim:
        c.start()

    arrive(3, 0)
    arrive(3, 1)
    for n in range(4):
        for k in range(PER):
            wedge[0, n, k] = ww[:, k, 8 + n, :]
            wedge[1, n, k] = ww[:, k, T + 4 + n, :]
    far = both(8, wedge, whalo)
    for c in far:
        c.start()
    for c in rim + far:
        c.wait()
    for n in range(2):
        for k in range(PER):
            ww[:, k, 6 + n, :] = whalo[0, 2 + n, k]
            ww[:, k, T + 8 + n, :] = whalo[1, n, k]
    for side in range(2):
        h = [whalo[side, n] for n in range(4)]
        e = [wedge[side, n] for n in range(4)]
        line = h + e[:2] if side == 0 else e[2:] + h
        mask = halo[0, side, PL : PL + 1, :]
        for n in range(2):
            x = line[n : n + 5]
            z = 0.625 * x[2] + 0.125 * (x[1] + x[3]) + 0.0625 * (x[0] + x[4])
            t = n - 2 if side == 0 else T + n
            r = qhalo[side, n] - 0.05 * (z * mask)
            for k in range(PER):
                r2[:, k, 8 + t, :] = r[k]

    for k in range(PER):
        arrive(3, 2 + k)

        def second_update(j, k=k):
            p = PER * j + k
            z = (
                0.625 * ww[j, k, 8 : T + 8]
                + 0.125 * (ww[j, k, 7 : T + 7] + ww[j, k, 9 : T + 9])
                + 0.0625 * (ww[j, k, 6 : T + 6] + ww[j, k, 10 : T + 10])
            )
            r2[j, k, 8 : T + 8] = n1[p] + ss[p] - 0.05 * (z * active)
            y = (
                0.625 * r2[j, k, 8 : T + 8]
                + 0.125 * (r2[j, k, 7 : T + 7] + r2[j, k, 9 : T + 9])
                + 0.0625 * (r2[j, k, 6 : T + 6] + r2[j, k, 10 : T + 10])
            )
            update = y * active
            last_update[p] = update
            new_state[p] = cur[p] - 0.05 * update

        planes(NI, 2, second_update)

    for c in layers + windows:
        c.wait_send()
    for unit in (1, 2, 3):
        gone(unit)


def local(n_dom, flow_state, donor_index, donor_weight, span_count):
    shape = (PL, T, S)
    padded = (PL, T + 16, S)
    pieces = (NI, PER, T, S)
    f32 = jnp.float32
    vmem = pl.BlockSpec(memory_space=pltpu.VMEM)
    anywhere = pl.BlockSpec(memory_space=pltpu.HBM)
    new_state, last_update = pl.pallas_call(
        functools.partial(kernel, n_dom, n_dom * T),
        out_shape=[jax.ShapeDtypeStruct(shape, f32)] * 2,
        in_specs=[anywhere] * 4,
        out_specs=[vmem, vmem],
        scratch_shapes=[
            pltpu.SMEM((2, T), jnp.int32),
            pltpu.SMEM((1,), jnp.int32),
            pltpu.VMEM((2, T), jnp.int32),
            pltpu.VMEM((2, T), f32),
            pltpu.VMEM(shape, f32),
            pltpu.VMEM(pieces, f32),
            pltpu.VMEM(pieces, f32),
            pltpu.VMEM(pieces, f32),
            pltpu.VMEM(pieces, f32),
            pltpu.VMEM(shape, f32),
            pltpu.VMEM((NI, PER, T + 16, S), f32),
            pltpu.VMEM(shape, f32),
            pltpu.VMEM(shape, f32),
            pltpu.VMEM(padded, f32),
            pltpu.VMEM(padded, f32),
            pltpu.VMEM(padded, f32),
            pltpu.VMEM((2, 3, T, S), f32),
            pltpu.VMEM((ITERS, 2, NV, 2 * T, S), f32),
            pltpu.VMEM((ITERS, 2, PL + 8, S), f32),
            pltpu.VMEM((ITERS, 2, PL + 8, S), f32),
            pltpu.VMEM((1, 2, 2, PL, S), f32),
            pltpu.VMEM((1, 2, 2, PL, S), f32),
            pltpu.VMEM((2, 2, PER, NI, S), f32),
            pltpu.VMEM((2, 2, PER, NI, S), f32),
            pltpu.VMEM((NI, PER, T + 16, S), f32),
            pltpu.VMEM((2, 4, PER, NI, S), f32),
            pltpu.VMEM((2, 4, PER, NI, S), f32),
            pltpu.SemaphoreType.DMA((5,)),
            pltpu.SemaphoreType.DMA((4,)),
            pltpu.SemaphoreType.DMA((4, 2 + PER)),
            pltpu.SemaphoreType.DMA((20,)),
            pltpu.SemaphoreType.DMA((20,)),
        ],
        compiler_params=pltpu.CompilerParams(
            collective_id=0, has_side_effects=True, vmem_limit_bytes=52 * 1024 * 1024
        ),
        cost_estimate=pl.CostEstimate(
            flops=20_000_000, bytes_accessed=3 * PL * T * S * 4, transcendentals=0
        ),
    )(flow_state.reshape(shape), donor_index[0], donor_weight[0], span_count)
    whole = (1, NV, AX, T, S)
    return new_state.reshape(whole), last_update.reshape(whole)


def solution(mesh):
    placed = (
        P("inst", None, None, "dom", None),
        P("inst", None, "dom"),
        P("inst", None, "dom"),
        P("dom"),
    )
    return jax.shard_map(
        functools.partial(local, mesh.shape["dom"]),
        mesh=mesh,
        in_specs=placed,
        out_specs=(P("inst", None, None, "dom", None), P("inst", None, None, "dom", None)),
        check_vma=False,
    )
```

time: 252 us -> 62.7 us (0.25)
  waiting for transfers between devices: 111 us -> 0 us
  Pallas kernels: 0 us -> 58.8 us
  local copies, waits for them, and re-layouts: 45.5 us -> 2.44 us
  starting transfers between devices: 31.1 us -> 0 us
  other arithmetic: 24 us -> 0 us
  matrix products: 23.6 us -> 0 us
  between operations: 15.9 us -> 1.3 us
    all_gather x2 -> x0, waiting for transfers between devices: 99 us -> none  [local(): lax.all_gather(current[None], 'inst', axis=0, tiled=True)]
    pallas_call x0 -> x1, Pallas kernels: none -> 58.8 us  [local(): pl.pallas_call(functools.partial(kernel, n_dom, n_dom * T), out_shape=[ja...]
    ppermute x16 -> x0, starting transfers between devices: 31 us -> none  [the longest x8 30.7 us: extended(): lax.ppermute(lax.slice_in_dim(block, 0, width, axis=dim), axis, backward)]
    dot_general x3 -> x0, matrix products: 23.6 us -> none  [the longest x2 22.8 us: local(): jnp.einsum('m,mvats->vats', own_row, lax.all_gather(current[None], 'inst'...]
    gather x8 -> x0, local copies, waits for them, and re-layouts: 16.7 us -> none  [the longest x4 9.04 us: interpolate(): near_take = jnp.take(donor_plane, donor_rows, axis=1)]
    slice x26 -> x0, local copies, waits for them, and re-layouts: 15.6 us -> none  [the longest x8 11.8 us: span_before(): return jnp.concatenate([values[..., :1], values[..., :-1]], axis=-1)]
    add x8 -> x0, other arithmetic: 11.3 us -> none  [the longest x2 6.32 us: local(): result = source + residual_terms(padded, ghost_after, ghost_before)]
    ppermute x16 -> x0, waiting for transfers between devices: 11.3 us -> none  [the longest x8 8.73 us: extended(): lax.ppermute(lax.slice_in_dim(block, block.shape[dim] - width, None, axis...]
  transfers between devices with their start and end apart: 18 -> 0, of which waited for: 11 -> 0; matrix products, arithmetic and copies ran while one was open for 23% -> 0% of each run, Pallas kernels for 0% -> 0%
where the time goes in v1:
time: 62.7 us; the launch traced here: 62.5 us
  Pallas kernels  58.8 us (94%)
  local copies, waits for them, and re-layouts  2.44 us (4%)
  between operations  1.3 us (2%)
    pallas_call x1, Pallas kernels, local(): pl.pallas_call(functools.partial(kernel, n_dom, n_dom * T), out_shape=[ja...  58.8 us
    unnamed x6, local copies, waits for them, and re-layouts  2.44 us

profile of v1, /device:TPU:0, one launch (start us, length us, event | category | flops | bytes accessed | tf_op | source)
XLA Modules:
  0.0 62.5 jit_solution(1900473708730301349)
XLA Ops:
  1.3 0.0 copy-start.1
  1.3 0.0 copy-start
  1.3 0.7 %copy-done.1 = f32[1,2,64]{2,1,0:T(2,128)S(1)} copy-done((f32[1,2,64]{2,1,0:T(2,128)S(1)}, f32[1,2,64]{2,1,0:T(2,128)}, u32[]{:S(2)}) %copy-start.1) | copy-done | bytes 536
  2.0 0.0 copy-done
  2.0 58.8 %shard_map.59 = (f32[24,64,128]{2,1,0:T(8,128)S(1)}, f32[24,64,128]{2,1,0:T(8,128)S(1)}) custom-call(f32[24,64,128]{2,1,0:T(8,128)} %bitcast.9, s32[2,64]{1,0:T(2,128)S(1)} %bitcast.7, f32[2,64]{1,0:T(2,128)S(1)} %bitcast.8, s32[1]{0:T(128)S(6)} %copy.8.count), custom_call_target="tpu_custom_call" | custom-call | flops 20000000 | bytes 2359296 | tf_op jit(solution)/shard_map/pallas_call | solution.py:503
  60.8 0.9 %copy.9 = f32[1,6,4,64,128]{4,3,2,1,0:T(8,128)} copy(f32[1,6,4,64,128]{4,3,2,1,0:T(8,128)S(1)} %bitcast.6) | data formatting | bytes 1572864
  61.6 0.9 %copy.10 = f32[1,6,4,64,128]{4,3,2,1,0:T(8,128)} copy(f32[1,6,4,64,128]{4,3,2,1,0:T(8,128)S(1)} %bitcast.5) | data formatting | bytes 1572864
Async XLA Ops:
  1.3 0.7 %copy-start.1 = (f32[1,2,64]{2,1,0:T(2,128)S(1)}, f32[1,2,64]{2,1,0:T(2,128)}, u32[]{:S(2)}) copy-start(f32[1,2,64]{2,1,0:T(2,128)} %param.6) | copy-start | bytes 1540
  1.3 0.7 %copy-start = (s32[1,2,64]{2,1,0:T(2,128)S(1)}, s32[1,2,64]{2,1,0:T(2,128)}, u32[]{:S(2)}) copy-start(s32[1,2,64]{2,1,0:T(2,128)} %param.5) | copy-start | bytes 1540

commit v2 on v1

v2 whole, which is shorter than its diff:
```python
import functools
import math

import jax
import jax.numpy as jnp
import numpy as np
from jax import lax
from jax.experimental import pallas as pl
from jax.experimental.pallas import tpu as pltpu
from jax.sharding import PartitionSpec as P

ITERS = 2
NI = 8
NV = 6
AX = 4
PL = NV * AX
T = 64
S = 128
ZN = 4
SLAB = T // ZN
ORDER = (1, 2, 0, 3)
MESH = pl.DeviceIdType.MESH


def spectral_row():
    k = np.arange(NI)[:, None] - np.arange(NI)[None, :]
    safe = np.where(k == 0, 1.0, np.sin(math.pi * k / NI))
    deriv = np.where(k == 0, 0.0, 0.5 * (-1.0) ** k * np.cos(math.pi * k / NI) / safe)
    return (deriv - 0.1 * deriv @ deriv)[:, 0]


def spectral_apply(x):
    row = spectral_row()
    even = [float(row[j] + row[j + 4]) / 2 for j in range(4)]
    odd = [float(row[j] - row[j + 4]) / 2 for j in range(4)]
    s = [x[z] + x[z + 4] for z in range(4)]
    d = [x[z] - x[z + 4] for z in range(4)]
    q0, q1 = s[0] - s[2], s[1] - s[3]
    s0 = even[0] * q0 + even[3] * q1
    s1 = even[1] * q0 + even[0] * q1
    sym = [s0, s1, -s0, -s1]
    out = [None] * NI
    for z in range(4):
        acc = None
        for y in range(4):
            coef = odd[z - y] if y <= z else -odd[4 + z - y]
            term = coef * d[y]
            acc = term if acc is None else acc + term
        out[z] = sym[z] + acc
        out[z + 4] = sym[z] - acc
    return out


def primitives(u):
    inv = 1.0 / u[0]
    vel = [u[1] * inv, u[2] * inv, u[3] * inv]
    nu = u[5] * inv
    pres = 0.4 * (u[4] - 0.5 * (u[1] * vel[0] + u[2] * vel[1] + u[3] * vel[2]))
    return vel, nu, pres


def centre_terms(u, vel, nu):
    return [
        0.1 * u[0],
        0.1 * u[1] + 0.02 * vel[0],
        0.1 * u[2] + 0.02 * vel[1],
        0.1 * u[3] + 0.02 * vel[2],
        0.1 * u[4],
        0.1 * u[5] + 0.02 * nu,
    ]


def half_flux(u, vel, pres, k):
    h = 0.5 * vel[k]
    f = [0.5 * u[1 + k], u[1] * h, u[2] * h, u[3] * h, (u[4] + pres) * h, u[5] * h]
    f[1 + k] = f[1 + k] + 0.5 * pres
    return f


def next_terms(u, k):
    vel, nu, pres = primitives(u)
    c = centre_terms(u, vel, nu)
    return [f - g for f, g in zip(half_flux(u, vel, pres, k), c)]


def prev_terms(u, k):
    vel, nu, pres = primitives(u)
    c = centre_terms(u, vel, nu)
    return [-(f + g) for f, g in zip(half_flux(u, vel, pres, k), c)]


def kernel(
    n_dom,
    n_cells,
    flow,
    idx,
    wgt,
    count,
    new_state,
    last_update,
    idx_s,
    count_s,
    idx_v,
    wgt_v,
    cur,
    in_u,
    in_n,
    w1,
    w2,
    ss,
    ww,
    n0,
    n1,
    rr,
    a2,
    b2,
    coef,
    win,
    edge,
    halo,
    redge,
    rhalo,
    qedge,
    qhalo,
    wedge,
    whalo,
    slab_n,
    slab_a,
    slab_b,
    slab_out,
    slab_in,
    load_sem,
    p_send,
    p_recv,
    d_send,
    d_recv,
):
    inst = lax.axis_index("inst")
    dom = lax.axis_index("dom")
    left = lax.rem(dom + n_dom - 1, n_dom)
    right = lax.rem(dom + 1, n_dom)

    def flip(d):
        return d + 2 - 4 * lax.rem(d // 2, 2)

    work = flip(dom)
    body, place = inst // ZN, lax.rem(inst, ZN)
    at_start = jnp.where(place == 0, 1, 0)
    at_end = jnp.where(place == ZN - 1, 1, 0)
    before = flip(lax.rem(work + n_dom - at_start, n_dom))
    beyond = flip(lax.rem(work + at_end, n_dom))
    below = (body * ZN + lax.rem(place + ZN - 1, ZN), before)
    above = (body * ZN + lax.rem(place + 1, ZN), beyond)

    loads = [
        pltpu.make_async_copy(source, target, load_sem.at[n])
        for n, (source, target) in enumerate(
            ((flow, cur), (idx, idx_s), (idx, idx_v), (wgt, wgt_v), (count, count_s))
        )
    ]
    for c in loads:
        c.start()
    barrier = pltpu.get_barrier_semaphore()
    for j in range(NI):
        pl.semaphore_signal(barrier, inc=1, device_id=(j, work), device_id_type=MESH)
    for device in ((inst, left), (inst, right), below, above):
        pl.semaphore_signal(barrier, inc=1, device_id=device, device_id_type=MESH)

    def remote(source, target, send, recv, device):
        return pltpu.make_async_remote_copy(
            src_ref=source,
            dst_ref=target,
            send_sem=send,
            recv_sem=recv,
            device_id=device,
            device_id_type=MESH,
        )

    def piece(unit, partner, part, slot):
        side, slab = partner // ZN, lax.rem(partner, ZN)
        row = 1 + side if part == 0 else (AX - 1) * side
        mine = pl.ds(pl.multiple_of(SLAB * slab, SLAB), SLAB)
        spot = 2 * part + slot // ZN
        at = SLAB * lax.rem(slot, ZN)
        if unit == 0:
            source, target = flow.at[:, row, mine], in_u.at[part, slot]
        elif unit == 1:
            source = w1.at[part, partner]
            target = ss.at[spot, :, pl.ds(pl.multiple_of(at, SLAB), SLAB)]
        elif unit == 2:
            source, target = n0.at[:, row, mine], in_n.at[slot]
        else:
            source = w2.at[part, partner]
            target = ww.at[spot, :, pl.ds(pl.multiple_of(at + 8, 8), SLAB)]
        return remote(source, target, p_send.at[unit], p_recv.at[unit, part], (partner, work))

    order = [lax.rem(inst + n, NI) for n in range(NI)]

    def send(unit, part):
        for j in order:
            piece(unit, j, part, inst).start()

    def arrive(unit, part):
        spots = pl.ds(2 * part, 2)
        ref = (in_u.at[part], ss.at[spots], in_n, ww.at[spots, :, pl.ds(8, T)])[unit]
        pltpu.make_async_copy(ref, ref, p_recv.at[unit, part]).wait()

    def gone(unit):
        ref = (flow, w1, n0.at[:, 1:3], w2)[unit]
        pltpu.make_async_copy(ref, ref, p_send.at[unit]).wait()

    def near(slot, source, target, device):
        return remote(source, target, d_send.at[slot], d_recv.at[slot], (inst, device))

    def both(slot, out, back):
        return [near(slot, out(0), back(1), left), near(slot + 1, out(1), back(0), right)]

    def start(copies):
        for c in copies:
            c.start()
        return copies

    def over(n, body):
        def step(i, _):
            body(i)
            return 0

        lax.fori_loop(0, n, step, 0)

    lane = lax.broadcasted_iota(jnp.int32, (8, S), 1)
    first_lane = lane == 0
    last_lane = lane == S - 1

    def spanwise(f, c):
        out = []
        for g, h in zip(f, c):
            up, down = g - h, g + h
            after = jnp.where(last_lane, up, pltpu.roll(up, S - 1, 1))
            prior = jnp.where(first_lane, down, pltpu.roll(down, 1, 1))
            out.append(6.0 * h + (after - prior))
        return out

    def spectral(part, target, plus=None):
        def variable(v):
            for t0 in range(0, SLAB, 8):
                rows = slice(t0, t0 + 8)
                if plus is None:
                    x = [in_u[part, m, v, rows, :] for m in range(NI)]
                else:
                    x = [w1[part, m, v, rows, :] + plus(m, v, t0) for m in range(NI)]
                for m, g in enumerate(spectral_apply(x)):
                    target[part, m, v, rows, :] = g

        over(NV, variable)

    def inside(out, first_tile, last_tile):
        def tile(i, _):
            t0 = pl.multiple_of(8 * i, 8)
            total = []
            first = []
            second = []
            for a in range(AX):
                u = [cur[v, a, pl.ds(t0, 8), :] for v in range(NV)]
                vel, nu, pres = primitives(u)
                c = centre_terms(u, vel, nu)
                f1 = half_flux(u, vel, pres, 0)
                first.append([f - g for f, g in zip(f1, c)])
                second.append([f + g for f, g in zip(f1, c)])
                f2 = half_flux(u, vel, pres, 1)
                for v in range(NV):
                    a2[v, a, pl.ds(t0 + 8, 8), :] = f2[v] - c[v]
                    b2[v, a, pl.ds(t0 + 8, 8), :] = f2[v] + c[v]
                total.append(spanwise(half_flux(u, vel, pres, 2), c))
            for a in range(AX):
                for v in range(NV):
                    r = total[a][v]
                    if a == AX - 1:
                        r = r + first[a][v]
                    elif a != AX // 2 - 1:
                        r = r + first[a + 1][v]
                    if a == 0:
                        r = r - second[a][v]
                    elif a != AX // 2:
                        r = r - second[a - 1][v]
                    out[v, a, pl.ds(t0, 8), :] = r
            return 0

        lax.fori_loop(first_tile, last_tile, tile, 0)

    def around(out, it, layers, windows):
        for c in layers:
            c.wait_recv()
        low = prev_terms([halo[it, 0, v] for v in range(NV)], 1)
        high = next_terms([halo[it, 1, v] for v in range(NV)], 1)
        for v in range(NV):
            for a in range(AX):
                b2[v, a, 7:8, :] = -low[v][a : a + 1]
                a2[v, a, T + 8 : T + 9, :] = high[v][a : a + 1]

        def variable(v):
            for a in range(AX):
                out[v, a] += a2[v, a, 9 : T + 9] - b2[v, a, 7 : T + 7]

        over(NV, variable)
        for c in windows:
            c.wait_recv()

        def ghosts(i):
            t0 = pl.multiple_of(8 * i, 8)
            for side in range(2):
                taps = [coef[side, n, pl.ds(t0, 8), :] for n in range(3)]
                u = []
                for v in range(NV):
                    g = taps[0] * win[it, side, v, pl.ds(base[side] + t0, 8), :]
                    g = g + taps[1] * win[it, side, v, pl.ds(base[side] + t0 + 1, 8), :]
                    g = g + taps[2] * win[it, side, v, pl.ds(base[side] + t0 + 2, 8), :]
                    u.append(g)
                terms = next_terms(u, 0) if side == 0 else prev_terms(u, 0)
                for v in range(NV):
                    out[v, 1 + side, pl.ds(t0, 8), :] += terms[v]

        over(T // 8, ghosts)

    def outer_layers(it):
        for side, t in enumerate((0, T - 1)):
            for v in range(NV):
                edge[it, side, v] = cur[v, :, t, :]
            edge[it, side, NV] = jnp.broadcast_to(active, (AX, S))
        return start(
            both(10 * it, lambda side: edge.at[it, side], lambda side: halo.at[it, side])
        )

    def interface_rows(it):
        for v in range(NV):
            win[it, 0, v, 0:T] = cur[v, 2]
            win[it, 1, v, T : 2 * T] = cur[v, 1]
        return start(
            [
                near(10 * it + 2, win.at[it, 0, :, 0:T], win.at[it, 0, :, T : 2 * T], left),
                near(10 * it + 3, win.at[it, 1, :, T : 2 * T], win.at[it, 1, :, 0:T], right),
            ]
        )

    def rim_of(slot, out, back, spots):
        return start(
            both(slot, lambda side: out.at[side, :, spots], lambda side: back.at[side, :, spots])
        )

    FRONT, REST = pl.ds(0, 2), pl.ds(2, 2)

    pl.semaphore_wait(barrier, NI + 4)
    for part in range(2):
        send(0, part)
    for c in loads:
        c.wait()
    active = jnp.where(lax.broadcasted_iota(jnp.int32, (1, S), 1) < count_s[0], 1.0, 0.0)
    layers = outer_layers(0)
    windows = interface_rows(0)

    def least(t, low):
        cell = dom * T + t
        gaps = (idx_s[0, t] - cell, cell - 1 - idx_s[1, t])
        gaps = [jnp.where(g < 0, g + n_cells, g) for g in gaps]
        return jnp.minimum(low[0], gaps[0]), jnp.minimum(low[1], gaps[1])

    most = (jnp.int32(n_cells), jnp.int32(n_cells))
    offset = [jnp.clip(x, 0, T - 2) for x in lax.fori_loop(0, T, least, most)]
    base = [offset[0], T - 2 - offset[1]]
    eye = lax.broadcasted_iota(jnp.int32, (T, T), 0) == lax.broadcasted_iota(
        jnp.int32, (T, T), 1
    )
    for side in range(2):
        cell = dom * T + lax.broadcasted_iota(jnp.int32, (1, T), 1)
        row = idx_v[side : side + 1, :]
        gap = row - cell if side == 0 else cell - 1 - row
        gap = jnp.where(gap < 0, gap + n_cells, gap)
        step = jnp.where(gap > offset[side], 1.0, 0.0)
        w = wgt_v[side : side + 1, :]
        taps = [(1.0 - step) * w, step * w + (1.0 - step) * (1.0 - w), step * (1.0 - w)]
        if side == 1:
            taps = [step * w, (1.0 - step) * w + step * (1.0 - w), (1.0 - step) * (1.0 - w)]
        for i, tap in enumerate(taps):
            column = jnp.sum(jnp.where(eye, tap, 0.0), axis=1, keepdims=True)
            coef[side, i] = jnp.broadcast_to(column, (T, S))

    half = T // 16
    inside(n0, 0, half)
    arrive(0, 0)
    spectral(0, w1)
    send(1, 0)
    arrive(0, 1)
    for v in range(NV):
        slab_out[0, v] = in_u[1, :, v, 0, :]
        slab_out[1, v] = in_u[1, :, v, SLAB - 1, :]
    slabs = start(
        [
            remote(slab_out.at[0], slab_in.at[1], d_send.at[18], d_recv.at[18], below),
            remote(slab_out.at[1], slab_in.at[0], d_send.at[19], d_recv.at[19], above),
        ]
    )
    spectral(1, w1)
    send(1, 1)
    inside(n0, half, 2 * half)
    around(n0, 0, layers, windows)
    send(2, 0)

    toward = jnp.where(body == 0, 1.0, -1.0)

    def slab_inside(m):
        for t0 in range(0, SLAB, 8):
            rows = slice(t0, t0 + 8)
            u = [in_u[0, m, v, rows, :] for v in range(NV)]
            vel, nu, pres = primitives(u)
            c1 = centre_terms(u, vel, nu)
            f1 = half_flux(u, vel, pres, 0)
            u = [in_u[1, m, v, rows, :] for v in range(NV)]
            vel, nu, pres = primitives(u)
            c = centre_terms(u, vel, nu)
            f = half_flux(u, vel, pres, 0)
            f2 = half_flux(u, vel, pres, 1)
            r = spanwise(half_flux(u, vel, pres, 2), c)
            for v in range(NV):
                slab_a[m, v, t0 : t0 + 8, :] = f2[v] - c[v]
                slab_b[m, v, t0 + 8 : t0 + 16, :] = f2[v] + c[v]
                slab_n[m, v, rows, :] = r[v] + (toward * (f1[v] - f[v]) - (c1[v] + c[v]))

    over(NI, slab_inside)
    for c in slabs:
        c.wait()
    low = prev_terms([slab_in[0, v] for v in range(NV)], 1)
    high = next_terms([slab_in[1, v] for v in range(NV)], 1)
    for v in range(NV):
        slab_b[:, v, 7, :] = -low[v]
        slab_a[:, v, SLAB, :] = high[v]

    def outer(m, v, t0):
        return slab_n[m, v, t0 : t0 + 8, :] + (
            slab_a[m, v, t0 + 1 : t0 + 9, :] - slab_b[m, v, t0 + 7 : t0 + 15, :]
        )

    spectral(1, w2, outer)
    send(3, 1)

    def keep_rows(out, spots, times, value):
        for spot in spots:
            for n, t in enumerate(times):
                out[n // (len(times) // 2), n % (len(times) // 2), spot] = value(spot, t)

    def put_rows(back, spots, times):
        for spot in spots:
            for n, t in enumerate(times):
                rr[spot, :, 8 + t, :] = back[n // 2, n % 2, spot]

    ends = (0, 1, T - 2, T - 1)
    outside = (-2, -1, T, T + 1)

    def smoothed(ref, spot, v):
        return (
            0.625 * ref[spot, v, 8 : T + 8]
            + 0.125 * (ref[spot, v, 7 : T + 7] + ref[spot, v, 9 : T + 9])
            + 0.0625 * (ref[spot, v, 6 : T + 6] + ref[spot, v, 10 : T + 10])
        )

    def sums(spots):
        def variable(v):
            for spot in spots:
                rr[spot, v, 8 : T + 8] = n0[v, ORDER[spot]] + ss[spot, v]

        over(NV, variable)

    def first_update(spots):
        def variable(v):
            for spot in spots:
                a = ORDER[spot]
                cur[v, a] = cur[v, a] - 0.05 * (smoothed(rr, spot, v) * active)

        over(NV, variable)

    def first_sum(spot, t):
        return n0[:, ORDER[spot], t, :] + ss[spot, :, t, :]

    arrive(1, 0)
    keep_rows(redge, (0, 1), ends, first_sum)
    rim = rim_of(4, redge, rhalo, FRONT)
    sums((0, 1))
    arrive(1, 1)
    keep_rows(redge, (2, 3), ends, first_sum)
    rim2 = rim_of(6, redge, rhalo, REST)
    for c in rim:
        c.wait()
    put_rows(rhalo, (0, 1), outside)
    gone(0)
    for c in layers + windows:
        c.wait_send()
    first_update((0, 1))
    windows = interface_rows(1)
    sums((2, 3))
    for c in rim2:
        c.wait()
    put_rows(rhalo, (2, 3), outside)
    first_update((2, 3))
    layers = outer_layers(1)

    arrive(2, 0)
    spectral(0, w2, lambda m, v, t0: in_n[m, v, t0 : t0 + 8, :])
    send(3, 0)
    inside(n1, 0, 2 * half)
    around(n1, 1, layers, windows)
    keep_rows(qedge, range(4), ends, lambda spot, t: n1[:, ORDER[spot], t, :] + ss[spot, :, t, :])
    rim = start(both(8, lambda side: qedge.at[side], lambda side: qhalo.at[side]))

    far_rows = (0, 1, 2, 3, T - 4, T - 3, T - 2, T - 1)

    def last_source(spot, t):
        return ww[spot, :, 8 + t, :]

    arrive(3, 1)
    keep_rows(wedge, (2, 3), far_rows, last_source)
    far2 = rim_of(14, wedge, whalo, REST)
    arrive(3, 0)
    keep_rows(wedge, (0, 1), far_rows, last_source)
    far = rim_of(16, wedge, whalo, FRONT)
    for c in rim:
        c.wait()

    def second_update(spots):
        for spot in spots:
            for n in range(2):
                ww[spot, :, 6 + n, :] = whalo[0, 2 + n, spot]
                ww[spot, :, T + 8 + n, :] = whalo[1, n, spot]
            for side in range(2):
                h = [whalo[side, n, spot] for n in range(4)]
                e = [wedge[side, n, spot] for n in range(4)]
                line = h + e[:2] if side == 0 else e[2:] + h
                mask = halo[0, side, NV, 0:1, :]
                for n in range(2):
                    x = line[n : n + 5]
                    z = 0.625 * x[2] + 0.125 * (x[1] + x[3]) + 0.0625 * (x[0] + x[4])
                    t = n - 2 if side == 0 else T + n
                    rr[spot, :, 8 + t, :] = qhalo[side, n, spot] - 0.05 * (z * mask)

        def variable(v):
            for spot in spots:
                a = ORDER[spot]
                rr[spot, v, 8 : T + 8] = (
                    n1[v, a] + ss[spot, v] - 0.05 * (smoothed(ww, spot, v) * active)
                )
                update = smoothed(rr, spot, v) * active
                last_update[v, a] = update
                new_state[v, a] = cur[v, a] - 0.05 * update

        over(NV, variable)

    for c in far2:
        c.wait()
    second_update((2, 3))
    for c in far:
        c.wait()
    second_update((0, 1))

    for c in layers + windows:
        c.wait_send()
    for unit in (1, 2, 3):
        gone(unit)


def local(n_dom, flow_state, donor_index, donor_weight, span_count):
    shape = (NV, AX, T, S)
    padded = (NV, AX, T + 16, S)
    pieces = (2, NI, NV, SLAB, S)
    turned = (AX, NV, T + 16, S)
    f32 = jnp.float32
    anywhere = pl.BlockSpec(memory_space=pl.ANY)
    vmem = pl.BlockSpec(memory_space=pltpu.VMEM)
    new_state, last_update = pl.pallas_call(
        functools.partial(kernel, n_dom, n_dom * T),
        out_shape=[jax.ShapeDtypeStruct(shape, f32)] * 2,
        in_specs=[anywhere] * 4,
        out_specs=[vmem, vmem],
        scratch_shapes=[
            pltpu.SMEM((2, T), jnp.int32),
            pltpu.SMEM((1,), jnp.int32),
            pltpu.VMEM((2, T), jnp.int32),
            pltpu.VMEM((2, T), f32),
            pltpu.VMEM(shape, f32),
            pltpu.VMEM(pieces, f32),
            pltpu.VMEM((NI, NV, SLAB, S), f32),
            pltpu.VMEM(pieces, f32),
            pltpu.VMEM(pieces, f32),
            pltpu.VMEM((AX, NV, T, S), f32),
            pltpu.VMEM(turned, f32),
            pltpu.VMEM(shape, f32),
            pltpu.VMEM(shape, f32),
            pltpu.VMEM(turned, f32),
            pltpu.VMEM(padded, f32),
            pltpu.VMEM(padded, f32),
            pltpu.VMEM((2, 3, T, S), f32),
            pltpu.VMEM((ITERS, 2, NV, 2 * T, S), f32),
            pltpu.VMEM((ITERS, 2, NV + 1, AX, S), f32),
            pltpu.VMEM((ITERS, 2, NV + 1, AX, S), f32),
            pltpu.VMEM((2, 2, AX, NV, S), f32),
            pltpu.VMEM((2, 2, AX, NV, S), f32),
            pltpu.VMEM((2, 2, AX, NV, S), f32),
            pltpu.VMEM((2, 2, AX, NV, S), f32),
            pltpu.VMEM((2, 4, AX, NV, S), f32),
            pltpu.VMEM((2, 4, AX, NV, S), f32),
            pltpu.VMEM((NI, NV, SLAB, S), f32),
            pltpu.VMEM((NI, NV, SLAB + 8, S), f32),
            pltpu.VMEM((NI, NV, SLAB + 8, S), f32),
            pltpu.VMEM((2, NV, NI, S), f32),
            pltpu.VMEM((2, NV, NI, S), f32),
            pltpu.SemaphoreType.DMA((5,)),
            pltpu.SemaphoreType.DMA((4,)),
            pltpu.SemaphoreType.DMA((4, 2)),
            pltpu.SemaphoreType.DMA((20,)),
            pltpu.SemaphoreType.DMA((20,)),
        ],
        compiler_params=pltpu.CompilerParams(
            collective_id=0, has_side_effects=True, vmem_limit_bytes=52 * 1024 * 1024
        ),
        cost_estimate=pl.CostEstimate(
            flops=20_000_000, bytes_accessed=3 * PL * T * S * 4, transcendentals=0
        ),
    )(flow_state.reshape(shape), donor_index[0], donor_weight[0], span_count)
    whole = (1, NV, AX, T, S)
    return new_state.reshape(whole), last_update.reshape(whole)


def solution(mesh):
    placed = (
        P("inst", None, None, "dom", None),
        P("inst", None, "dom"),
        P("inst", None, "dom"),
        P("dom"),
    )
    return jax.shard_map(
        functools.partial(local, mesh.shape["dom"]),
        mesh=mesh,
        in_specs=placed,
        out_specs=(P("inst", None, None, "dom", None), P("inst", None, None, "dom", None)),
        check_vma=False,
    )
```

time: 62.7 us -> 58.2 us (0.928)
  Pallas kernels: 58.8 us -> 54 us
    pallas_call x1, Pallas kernels: 58.8 us -> 54 us  [local(): pl.pallas_call(functools.partial(kernel, n_dom, n_dom * T), out_shape=[ja...]
where the time goes in v2:
time: 58.2 us; the launch traced here: 57.8 us
  Pallas kernels  54 us (93%)
  local copies, waits for them, and re-layouts  2.44 us (4%)
  between operations  1.3 us (2%)
    pallas_call x1, Pallas kernels, local(): pl.pallas_call(functools.partial(kernel, n_dom, n_dom * T), out_shape=[ja...  54 us
    unnamed x6, local copies, waits for them, and re-layouts  2.44 us

profile of v2, /device:TPU:0, one launch (start us, length us, event | category | flops | bytes accessed | tf_op | source)
XLA Modules:
  0.0 57.8 jit_solution(12084389675009317850)
XLA Ops:
  1.3 0.0 copy-start.1
  1.3 0.0 copy-start
  1.3 0.7 %copy-done.1 = f32[1,2,64]{2,1,0:T(2,128)S(1)} copy-done((f32[1,2,64]{2,1,0:T(2,128)S(1)}, f32[1,2,64]{2,1,0:T(2,128)}, u32[]{:S(2)}) %copy-start.1) | copy-done | bytes 536
  2.0 0.0 copy-done
  2.0 54.0 %shard_map.59 = (f32[6,4,64,128]{3,2,1,0:T(8,128)S(1)}, f32[6,4,64,128]{3,2,1,0:T(8,128)S(1)}) custom-call(f32[6,4,64,128]{3,2,1,0:T(8,128)} %bitcast.9, s32[2,64]{1,0:T(2,128)S(1)} %bitcast.7, f32[2,64]{1,0:T(2,128)S(1)} %bitcast.8, s32[1]{0:T(128)S(6)} %copy.8.count), custom_call_target="tpu_custom_call" | custom-call | flops 20000000 | bytes 2359296 | tf_op jit(solution)/shard_map/pallas_call | solution.py:575
  56.0 0.9 %copy.9 = f32[1,6,4,64,128]{4,3,2,1,0:T(8,128)} copy(f32[1,6,4,64,128]{4,3,2,1,0:T(8,128)S(1)} %bitcast.6) | data formatting | bytes 1572864
  56.9 0.9 %copy.10 = f32[1,6,4,64,128]{4,3,2,1,0:T(8,128)} copy(f32[1,6,4,64,128]{4,3,2,1,0:T(8,128)S(1)} %bitcast.5) | data formatting | bytes 1572864
Async XLA Ops:
  1.3 0.7 %copy-start.1 = (f32[1,2,64]{2,1,0:T(2,128)S(1)}, f32[1,2,64]{2,1,0:T(2,128)}, u32[]{:S(2)}) copy-start(f32[1,2,64]{2,1,0:T(2,128)} %param.6) | copy-start | bytes 1540
  1.3 0.7 %copy-start = (s32[1,2,64]{2,1,0:T(2,128)S(1)}, s32[1,2,64]{2,1,0:T(2,128)}, u32[]{:S(2)}) copy-start(s32[1,2,64]{2,1,0:T(2,128)} %param.5) | copy-start | bytes 1540

commit v3 on v2

--- a/solution.py
+++ b/solution.py
@@ -132,6 +132,8 @@
     load_sem,
     p_send,
     p_recv,
+    h_send,
+    h_recv,
     d_send,
     d_recv,
 ):
@@ -163,7 +165,10 @@
     barrier = pltpu.get_barrier_semaphore()
     for j in range(NI):
         pl.semaphore_signal(barrier, inc=1, device_id=(j, work), device_id_type=MESH)
-    for device in ((inst, left), (inst, right), below, above):
+    friends = [(inst, left), (inst, right), below, above]
+    for side in range(2):
+        friends += [(side * ZN + ZN - 1, flip(left)), (side * ZN, flip(right))]
+    for device in friends:
         pl.semaphore_signal(barrier, inc=1, device_id=device, device_id_type=MESH)
 
     def remote(source, target, send, recv, device):
@@ -208,6 +213,39 @@
     def gone(unit):
         ref = (flow, w1, n0.at[:, 1:3], w2)[unit]
         pltpu.make_async_copy(ref, ref, p_send.at[unit]).wait()
+
+    end_row = (SLAB - 4) * at_end
+
+    def send_ends(part):
+        def instance(m):
+            for v in range(NV):
+                wedge[part, m, v] = w2[part, m, v, pl.ds(end_row, 4), :]
+
+        over(NI, instance)
+        for at_edge, side, block in ((at_start, 1, before), (at_end, 0, beyond)):
+
+            @pl.when(at_edge == 1)
+            def _(side=side, block=block):
+                for m in order:
+                    remote(
+                        wedge.at[part, m],
+                        whalo.at[side, 2 * part + body],
+                        h_send.at[part],
+                        h_recv.at[part, side],
+                        (m, flip(block)),
+                    ).start()
+
+    def ends_came(part):
+        for side in range(2):
+            ref = whalo.at[side, pl.ds(2 * part, 2)]
+            pltpu.make_async_copy(ref, ref, h_recv.at[part, side]).wait()
+
+    def ends_gone():
+        @pl.when(at_start + at_end == 1)
+        def _():
+            for part in range(2):
+                ref = wedge.at[part]
+                pltpu.make_async_copy(ref, ref, h_send.at[part]).wait()
 
     def near(slot, source, target, device):
         return remote(source, target, d_send.at[slot], d_recv.at[slot], (inst, device))
@@ -348,7 +386,7 @@
 
     FRONT, REST = pl.ds(0, 2), pl.ds(2, 2)
 
-    pl.semaphore_wait(barrier, NI + 4)
+    pl.semaphore_wait(barrier, NI + 4 + NI * (at_start + at_end))
     for part in range(2):
         send(0, part)
     for c in loads:
@@ -439,6 +477,7 @@
         )
 
     spectral(1, w2, outer)
+    send_ends(1)
     send(3, 1)
 
     def keep_rows(out, spots, times, value):
@@ -503,35 +542,25 @@
 
     arrive(2, 0)
     spectral(0, w2, lambda m, v, t0: in_n[m, v, t0 : t0 + 8, :])
+    send_ends(0)
     send(3, 0)
     inside(n1, 0, 2 * half)
     around(n1, 1, layers, windows)
     keep_rows(qedge, range(4), ends, lambda spot, t: n1[:, ORDER[spot], t, :] + ss[spot, :, t, :])
     rim = start(both(8, lambda side: qedge.at[side], lambda side: qhalo.at[side]))
 
-    far_rows = (0, 1, 2, 3, T - 4, T - 3, T - 2, T - 1)
-
-    def last_source(spot, t):
-        return ww[spot, :, 8 + t, :]
-
-    arrive(3, 1)
-    keep_rows(wedge, (2, 3), far_rows, last_source)
-    far2 = rim_of(14, wedge, whalo, REST)
-    arrive(3, 0)
-    keep_rows(wedge, (0, 1), far_rows, last_source)
-    far = rim_of(16, wedge, whalo, FRONT)
     for c in rim:
         c.wait()
 
     def second_update(spots):
         for spot in spots:
             for n in range(2):
-                ww[spot, :, 6 + n, :] = whalo[0, 2 + n, spot]
-                ww[spot, :, T + 8 + n, :] = whalo[1, n, spot]
+                ww[spot, :, 6 + n, :] = whalo[0, spot, :, 2 + n, :]
+                ww[spot, :, T + 8 + n, :] = whalo[1, spot, :, n, :]
             for side in range(2):
-                h = [whalo[side, n, spot] for n in range(4)]
-                e = [wedge[side, n, spot] for n in range(4)]
-                line = h + e[:2] if side == 0 else e[2:] + h
+                h = [whalo[side, spot, :, n, :] for n in range(4)]
+                e = [ww[spot, :, 8 + t, :] for t in ((0, 1), (T - 2, T - 1))[side]]
+                line = h + e if side == 0 else e + h
                 mask = halo[0, side, NV, 0:1, :]
                 for n in range(2):
                     x = line[n : n + 5]
@@ -551,17 +580,16 @@
 
         over(NV, variable)
 
-    for c in far2:
-        c.wait()
-    second_update((2, 3))
-    for c in far:
-        c.wait()
-    second_update((0, 1))
+    for part in (1, 0):
+        arrive(3, part)
+        ends_came(part)
+        second_update((2 * part, 2 * part + 1))
 
     for c in layers + windows:
         c.wait_send()
     for unit in (1, 2, 3):
         gone(unit)
+    ends_gone()
 
 
 def local(n_dom, flow_state, donor_index, donor_weight, span_count):
@@ -602,8 +630,8 @@
             pltpu.VMEM((2, 2, AX, NV, S), f32),
             pltpu.VMEM((2, 2, AX, NV, S), f32),
             pltpu.VMEM((2, 2, AX, NV, S), f32),
-            pltpu.VMEM((2, 4, AX, NV, S), f32),
-            pltpu.VMEM((2, 4, AX, NV, S), f32),
+            pltpu.VMEM((2, NI, NV, 4, S), f32),
+            pltpu.VMEM((2, AX, NV, 4, S), f32),
             pltpu.VMEM((NI, NV, SLAB, S), f32),
             pltpu.VMEM((NI, NV, SLAB + 8, S), f32),
             pltpu.VMEM((NI, NV, SLAB + 8, S), f32),
@@ -612,6 +640,8 @@
             pltpu.SemaphoreType.DMA((5,)),
             pltpu.SemaphoreType.DMA((4,)),
             pltpu.SemaphoreType.DMA((4, 2)),
+            pltpu.SemaphoreType.DMA((2,)),
+            pltpu.SemaphoreType.DMA((2, 2)),
             pltpu.SemaphoreType.DMA((20,)),
             pltpu.SemaphoreType.DMA((20,)),
         ],

time: 58.2 us -> 59.5 us (1.022)
  Pallas kernels: 54 us -> 55.4 us
    pallas_call x1, Pallas kernels: 54 us -> 55.4 us  [local(): pl.pallas_call(functools.partial(kernel, n_dom, n_dom * T), out_shape=[ja...]
where the time goes in v3:
time: 59.5 us; the launch traced here: 59.1 us
  Pallas kernels  55.4 us (93%)
  local copies, waits for them, and re-layouts  2.44 us (4%)
  between operations  1.3 us (2%)
    pallas_call x1, Pallas kernels, local(): pl.pallas_call(functools.partial(kernel, n_dom, n_dom * T), out_shape=[ja...  55.4 us
    unnamed x6, local copies, waits for them, and re-layouts  2.44 us

profile of v3, /device:TPU:0, one launch (start us, length us, event | category | flops | bytes accessed | tf_op | source)
XLA Modules:
  0.0 59.1 jit_solution(9952313075771512259)
XLA Ops:
  1.3 0.0 copy-start.1
  1.3 0.0 copy-start
  1.3 0.7 %copy-done.1 = f32[1,2,64]{2,1,0:T(2,128)S(1)} copy-done((f32[1,2,64]{2,1,0:T(2,128)S(1)}, f32[1,2,64]{2,1,0:T(2,128)}, u32[]{:S(2)}) %copy-start.1) | copy-done | bytes 536
  2.0 0.0 copy-done
  2.0 55.4 %shard_map.59 = (f32[6,4,64,128]{3,2,1,0:T(8,128)S(1)}, f32[6,4,64,128]{3,2,1,0:T(8,128)S(1)}) custom-call(f32[6,4,64,128]{3,2,1,0:T(8,128)} %bitcast.9, s32[2,64]{1,0:T(2,128)S(1)} %bitcast.7, f32[2,64]{1,0:T(2,128)S(1)} %bitcast.8, s32[1]{0:T(128)S(6)} %copy.8.count), custom_call_target="tpu_custom_call" | custom-call | flops 20000000 | bytes 2359296 | tf_op jit(solution)/shard_map/pallas_call | solution.py:603
  57.4 0.9 %copy.9 = f32[1,6,4,64,128]{4,3,2,1,0:T(8,128)} copy(f32[1,6,4,64,128]{4,3,2,1,0:T(8,128)S(1)} %bitcast.6) | data formatting | bytes 1572864
  58.2 0.9 %copy.10 = f32[1,6,4,64,128]{4,3,2,1,0:T(8,128)} copy(f32[1,6,4,64,128]{4,3,2,1,0:T(8,128)S(1)} %bitcast.5) | data formatting | bytes 1572864
Async XLA Ops:
  1.3 0.7 %copy-start.1 = (f32[1,2,64]{2,1,0:T(2,128)S(1)}, f32[1,2,64]{2,1,0:T(2,128)}, u32[]{:S(2)}) copy-start(f32[1,2,64]{2,1,0:T(2,128)} %param.6) | copy-start | bytes 1540
  1.3 0.7 %copy-start = (s32[1,2,64]{2,1,0:T(2,128)S(1)}, s32[1,2,64]{2,1,0:T(2,128)}, u32[]{:S(2)}) copy-start(s32[1,2,64]{2,1,0:T(2,128)} %param.5) | copy-start | bytes 1540

commit v4 on v2

--- a/solution.py
+++ b/solution.py
@@ -287,7 +287,7 @@
 
         lax.fori_loop(first_tile, last_tile, tile, 0)
 
-    def around(out, it, layers, windows):
+    def around(out, it, layers):
         for c in layers:
             c.wait_recv()
         low = prev_terms([halo[it, 0, v] for v in range(NV)], 1)
@@ -302,6 +302,8 @@
                 out[v, a] += a2[v, a, 9 : T + 9] - b2[v, a, 7 : T + 7]
 
         over(NV, variable)
+
+    def interface(out, it, windows):
         for c in windows:
             c.wait_recv()
 
@@ -401,7 +403,8 @@
     spectral(1, w1)
     send(1, 1)
     inside(n0, half, 2 * half)
-    around(n0, 0, layers, windows)
+    around(n0, 0, layers)
+    interface(n0, 0, windows)
     send(2, 0)
 
     toward = jnp.where(body == 0, 1.0, -1.0)
@@ -439,7 +442,6 @@
         )
 
     spectral(1, w2, outer)
-    send(3, 1)
 
     def keep_rows(out, spots, times, value):
         for spot in spots:
@@ -494,6 +496,7 @@
         c.wait_send()
     first_update((0, 1))
     windows = interface_rows(1)
+    send(3, 1)
     sums((2, 3))
     for c in rim2:
         c.wait()
@@ -505,9 +508,16 @@
     spectral(0, w2, lambda m, v, t0: in_n[m, v, t0 : t0 + 8, :])
     send(3, 0)
     inside(n1, 0, 2 * half)
-    around(n1, 1, layers, windows)
-    keep_rows(qedge, range(4), ends, lambda spot, t: n1[:, ORDER[spot], t, :] + ss[spot, :, t, :])
-    rim = start(both(8, lambda side: qedge.at[side], lambda side: qhalo.at[side]))
+    around(n1, 1, layers)
+
+    def second_sum(spot, t):
+        return n1[:, ORDER[spot], t, :] + ss[spot, :, t, :]
+
+    keep_rows(qedge, (2, 3), ends, second_sum)
+    rim2 = rim_of(8, qedge, qhalo, REST)
+    interface(n1, 1, windows)
+    keep_rows(qedge, (0, 1), ends, second_sum)
+    rim = rim_of(12 + 2, qedge, qhalo, FRONT)
 
     far_rows = (0, 1, 2, 3, T - 4, T - 3, T - 2, T - 1)
 
@@ -516,12 +526,10 @@
 
     arrive(3, 1)
     keep_rows(wedge, (2, 3), far_rows, last_source)
-    far2 = rim_of(14, wedge, whalo, REST)
+    far2 = rim_of(16, wedge, whalo, REST)
     arrive(3, 0)
     keep_rows(wedge, (0, 1), far_rows, last_source)
-    far = rim_of(16, wedge, whalo, FRONT)
-    for c in rim:
-        c.wait()
+    far = rim_of(20, wedge, whalo, FRONT)
 
     def second_update(spots):
         for spot in spots:
@@ -551,10 +559,10 @@
 
         over(NV, variable)
 
-    for c in far2:
+    for c in rim2 + far2:
         c.wait()
     second_update((2, 3))
-    for c in far:
+    for c in rim + far:
         c.wait()
     second_update((0, 1))
 
@@ -612,8 +620,8 @@
             pltpu.SemaphoreType.DMA((5,)),
             pltpu.SemaphoreType.DMA((4,)),
             pltpu.SemaphoreType.DMA((4, 2)),
-            pltpu.SemaphoreType.DMA((20,)),
-            pltpu.SemaphoreType.DMA((20,)),
+            pltpu.SemaphoreType.DMA((22,)),
+            pltpu.SemaphoreType.DMA((22,)),
         ],
         compiler_params=pltpu.CompilerParams(
             collective_id=0, has_side_effects=True, vmem_limit_bytes=52 * 1024 * 1024

time: 58.2 us -> 58.5 us (level)
  Pallas kernels: 54 us -> 54.6 us
where the time goes in v4:
time: 58.5 us; the launch traced here: 58.3 us
  Pallas kernels  54.6 us (93%)
  local copies, waits for them, and re-layouts  2.44 us (4%)
  between operations  1.3 us (2%)
    pallas_call x1, Pallas kernels, local(): pl.pallas_call(functools.partial(kernel, n_dom, n_dom * T), out_shape=[ja...  54.6 us
    unnamed x6, local copies, waits for them, and re-layouts  2.44 us

profile of v4, /device:TPU:0, one launch (start us, length us, event | category | flops | bytes accessed | tf_op | source)
XLA Modules:
  0.0 58.3 jit_solution(5179876838657722371)
XLA Ops:
  1.3 0.0 copy-start.1
  1.3 0.0 copy-start
  1.3 0.7 %copy-done.1 = f32[1,2,64]{2,1,0:T(2,128)S(1)} copy-done((f32[1,2,64]{2,1,0:T(2,128)S(1)}, f32[1,2,64]{2,1,0:T(2,128)}, u32[]{:S(2)}) %copy-start.1) | copy-done | bytes 536
  2.0 0.0 copy-done
  2.0 54.6 %shard_map.59 = (f32[6,4,64,128]{3,2,1,0:T(8,128)S(1)}, f32[6,4,64,128]{3,2,1,0:T(8,128)S(1)}) custom-call(f32[6,4,64,128]{3,2,1,0:T(8,128)} %bitcast.9, s32[2,64]{1,0:T(2,128)S(1)} %bitcast.7, f32[2,64]{1,0:T(2,128)S(1)} %bitcast.8, s32[1]{0:T(128)S(6)} %copy.8.count), custom_call_target="tpu_custom_call" | custom-call | flops 20000000 | bytes 2359296 | tf_op jit(solution)/shard_map/pallas_call | solution.py:583
  56.6 0.9 %copy.9 = f32[1,6,4,64,128]{4,3,2,1,0:T(8,128)} copy(f32[1,6,4,64,128]{4,3,2,1,0:T(8,128)S(1)} %bitcast.6) | data formatting | bytes 1572864
  57.5 0.9 %copy.10 = f32[1,6,4,64,128]{4,3,2,1,0:T(8,128)} copy(f32[1,6,4,64,128]{4,3,2,1,0:T(8,128)S(1)} %bitcast.5) | data formatting | bytes 1572864
Async XLA Ops:
  1.3 0.7 %copy-start.1 = (f32[1,2,64]{2,1,0:T(2,128)S(1)}, f32[1,2,64]{2,1,0:T(2,128)}, u32[]{:S(2)}) copy-start(f32[1,2,64]{2,1,0:T(2,128)} %param.6) | copy-start | bytes 1540
  1.3 0.7 %copy-start = (s32[1,2,64]{2,1,0:T(2,128)S(1)}, s32[1,2,64]{2,1,0:T(2,128)}, u32[]{:S(2)}) copy-start(s32[1,2,64]{2,1,0:T(2,128)} %param.5) | copy-start | bytes 1540

commit v5 on v4

--- a/solution.py
+++ b/solution.py
@@ -344,9 +344,7 @@
         )
 
     def rim_of(slot, out, back, spots):
-        return start(
-            both(slot, lambda side: out.at[side, :, spots], lambda side: back.at[side, :, spots])
-        )
+        return start(both(slot, lambda side: out.at[side, spots], lambda side: back.at[side, spots]))
 
     FRONT, REST = pl.ds(0, 2), pl.ds(2, 2)
 
@@ -443,18 +441,18 @@
 
     spectral(1, w2, outer)
 
-    def keep_rows(out, spots, times, value):
+    def keep_rows(out, spots, value):
+        n = out.shape[3]
         for spot in spots:
-            for n, t in enumerate(times):
-                out[n // (len(times) // 2), n % (len(times) // 2), spot] = value(spot, t)
-
-    def put_rows(back, spots, times):
+            for v in range(NV):
+                out[0, spot, v] = value(spot, v, 0, n)
+                out[1, spot, v] = value(spot, v, T - n, T)
+
+    def put_rows(back, spots):
         for spot in spots:
-            for n, t in enumerate(times):
-                rr[spot, :, 8 + t, :] = back[n // 2, n % 2, spot]
-
-    ends = (0, 1, T - 2, T - 1)
-    outside = (-2, -1, T, T + 1)
+            for v in range(NV):
+                rr[spot, v, 6:8, :] = back[0, spot, v]
+                rr[spot, v, T + 8 : T + 10, :] = back[1, spot, v]
 
     def smoothed(ref, spot, v):
         return (
@@ -478,19 +476,19 @@
 
         over(NV, variable)
 
-    def first_sum(spot, t):
-        return n0[:, ORDER[spot], t, :] + ss[spot, :, t, :]
+    def first_sum(spot, v, t0, t1):
+        return n0[v, ORDER[spot], t0:t1, :] + ss[spot, v, t0:t1, :]
 
     arrive(1, 0)
-    keep_rows(redge, (0, 1), ends, first_sum)
+    keep_rows(redge, (0, 1), first_sum)
     rim = rim_of(4, redge, rhalo, FRONT)
     sums((0, 1))
     arrive(1, 1)
-    keep_rows(redge, (2, 3), ends, first_sum)
+    keep_rows(redge, (2, 3), first_sum)
     rim2 = rim_of(6, redge, rhalo, REST)
     for c in rim:
         c.wait()
-    put_rows(rhalo, (0, 1), outside)
+    put_rows(rhalo, (0, 1))
     gone(0)
     for c in layers + windows:
         c.wait_send()
@@ -500,7 +498,7 @@
     sums((2, 3))
     for c in rim2:
         c.wait()
-    put_rows(rhalo, (2, 3), outside)
+    put_rows(rhalo, (2, 3))
     first_update((2, 3))
     layers = outer_layers(1)
 
@@ -510,46 +508,40 @@
     inside(n1, 0, 2 * half)
     around(n1, 1, layers)
 
-    def second_sum(spot, t):
-        return n1[:, ORDER[spot], t, :] + ss[spot, :, t, :]
-
-    keep_rows(qedge, (2, 3), ends, second_sum)
+    def second_sum(spot, v, t0, t1):
+        return n1[v, ORDER[spot], t0:t1, :] + ss[spot, v, t0:t1, :]
+
+    keep_rows(qedge, (2, 3), second_sum)
     rim2 = rim_of(8, qedge, qhalo, REST)
     interface(n1, 1, windows)
-    keep_rows(qedge, (0, 1), ends, second_sum)
+    keep_rows(qedge, (0, 1), second_sum)
     rim = rim_of(12 + 2, qedge, qhalo, FRONT)
 
-    far_rows = (0, 1, 2, 3, T - 4, T - 3, T - 2, T - 1)
-
-    def last_source(spot, t):
-        return ww[spot, :, 8 + t, :]
+    def last_source(spot, v, t0, t1):
+        return ww[spot, v, 8 + t0 : 8 + t1, :]
 
     arrive(3, 1)
-    keep_rows(wedge, (2, 3), far_rows, last_source)
+    keep_rows(wedge, (2, 3), last_source)
     far2 = rim_of(16, wedge, whalo, REST)
     arrive(3, 0)
-    keep_rows(wedge, (0, 1), far_rows, last_source)
+    keep_rows(wedge, (0, 1), last_source)
     far = rim_of(20, wedge, whalo, FRONT)
 
+    masks = [halo[0, side, NV, 0:1, :] for side in range(2)]
+
     def second_update(spots):
-        for spot in spots:
-            for n in range(2):
-                ww[spot, :, 6 + n, :] = whalo[0, 2 + n, spot]
-                ww[spot, :, T + 8 + n, :] = whalo[1, n, spot]
-            for side in range(2):
-                h = [whalo[side, n, spot] for n in range(4)]
-                e = [wedge[side, n, spot] for n in range(4)]
-                line = h + e[:2] if side == 0 else e[2:] + h
-                mask = halo[0, side, NV, 0:1, :]
-                for n in range(2):
-                    x = line[n : n + 5]
-                    z = 0.625 * x[2] + 0.125 * (x[1] + x[3]) + 0.0625 * (x[0] + x[4])
-                    t = n - 2 if side == 0 else T + n
-                    rr[spot, :, 8 + t, :] = qhalo[side, n, spot] - 0.05 * (z * mask)
-
         def variable(v):
             for spot in spots:
                 a = ORDER[spot]
+                ww[spot, v, 4:8, :] = whalo[0, spot, v]
+                ww[spot, v, T + 8 : T + 12, :] = whalo[1, spot, v]
+                for side, t in enumerate((6, T + 8)):
+                    z = (
+                        0.625 * ww[spot, v, t : t + 2, :]
+                        + 0.125 * (ww[spot, v, t - 1 : t + 1, :] + ww[spot, v, t + 1 : t + 3, :])
+                        + 0.0625 * (ww[spot, v, t - 2 : t, :] + ww[spot, v, t + 2 : t + 4, :])
+                    )
+                    rr[spot, v, t : t + 2, :] = qhalo[side, spot, v] - 0.05 * (z * masks[side])
                 rr[spot, v, 8 : T + 8] = (
                     n1[v, a] + ss[spot, v] - 0.05 * (smoothed(ww, spot, v) * active)
                 )
@@ -606,12 +598,12 @@
             pltpu.VMEM((ITERS, 2, NV, 2 * T, S), f32),
             pltpu.VMEM((ITERS, 2, NV + 1, AX, S), f32),
             pltpu.VMEM((ITERS, 2, NV + 1, AX, S), f32),
-            pltpu.VMEM((2, 2, AX, NV, S), f32),
-            pltpu.VMEM((2, 2, AX, NV, S), f32),
-            pltpu.VMEM((2, 2, AX, NV, S), f32),
-            pltpu.VMEM((2, 2, AX, NV, S), f32),
-            pltpu.VMEM((2, 4, AX, NV, S), f32),
-            pltpu.VMEM((2, 4, AX, NV, S), f32),
+            pltpu.VMEM((2, AX, NV, 2, S), f32),
+            pltpu.VMEM((2, AX, NV, 2, S), f32),
+            pltpu.VMEM((2, AX, NV, 2, S), f32),
+            pltpu.VMEM((2, AX, NV, 2, S), f32),
+            pltpu.VMEM((2, AX, NV, 4, S), f32),
+            pltpu.VMEM((2, AX, NV, 4, S), f32),
             pltpu.VMEM((NI, NV, SLAB, S), f32),
             pltpu.VMEM((NI, NV, SLAB + 8, S), f32),
             pltpu.VMEM((NI, NV, SLAB + 8, S), f32),

time: 58.5 us -> 58.5 us (level)
  no operation moved by 1% of the time
where the time goes in v5:
time: 58.5 us; the launch traced here: 58.3 us
  Pallas kernels  54.6 us (93%)
  local copies, waits for them, and re-layouts  2.44 us (4%)
  between operations  1.3 us (2%)
    pallas_call x1, Pallas kernels, local(): pl.pallas_call(functools.partial(kernel, n_dom, n_dom * T), out_shape=[ja...  54.6 us
    unnamed x6, local copies, waits for them, and re-layouts  2.44 us

profile of v5, /device:TPU:0, one launch (start us, length us, event | category | flops | bytes accessed | tf_op | source)
XLA Modules:
  0.0 58.3 jit_solution(14128332183303462422)
XLA Ops:
  1.3 0.0 copy-start.1
  1.3 0.0 copy-start
  1.3 0.7 %copy-done.1 = f32[1,2,64]{2,1,0:T(2,128)S(1)} copy-done((f32[1,2,64]{2,1,0:T(2,128)S(1)}, f32[1,2,64]{2,1,0:T(2,128)}, u32[]{:S(2)}) %copy-start.1) | copy-done | bytes 536
  2.0 0.0 copy-done
  2.0 54.6 %shard_map.59 = (f32[6,4,64,128]{3,2,1,0:T(8,128)S(1)}, f32[6,4,64,128]{3,2,1,0:T(8,128)S(1)}) custom-call(f32[6,4,64,128]{3,2,1,0:T(8,128)} %bitcast.9, s32[2,64]{1,0:T(2,128)S(1)} %bitcast.7, f32[2,64]{1,0:T(2,128)S(1)} %bitcast.8, s32[1]{0:T(128)S(6)} %copy.8.count), custom_call_target="tpu_custom_call" | custom-call | flops 20000000 | bytes 2359296 | tf_op jit(solution)/shard_map/pallas_call | solution.py:575
  56.6 0.9 %copy.9 = f32[1,6,4,64,128]{4,3,2,1,0:T(8,128)} copy(f32[1,6,4,64,128]{4,3,2,1,0:T(8,128)S(1)} %bitcast.6) | data formatting | bytes 1572864
  57.4 0.9 %copy.10 = f32[1,6,4,64,128]{4,3,2,1,0:T(8,128)} copy(f32[1,6,4,64,128]{4,3,2,1,0:T(8,128)S(1)} %bitcast.5) | data formatting | bytes 1572864
Async XLA Ops:
  1.3 0.7 %copy-start.1 = (f32[1,2,64]{2,1,0:T(2,128)S(1)}, f32[1,2,64]{2,1,0:T(2,128)}, u32[]{:S(2)}) copy-start(f32[1,2,64]{2,1,0:T(2,128)} %param.6) | copy-start | bytes 1540
  1.3 0.7 %copy-start = (s32[1,2,64]{2,1,0:T(2,128)S(1)}, s32[1,2,64]{2,1,0:T(2,128)}, u32[]{:S(2)}) copy-start(s32[1,2,64]{2,1,0:T(2,128)} %param.5) | copy-start | bytes 1540

commit v6 on v5

--- a/solution.py
+++ b/solution.py
@@ -132,6 +132,7 @@
     load_sem,
     p_send,
     p_recv,
+    f_send,
     d_send,
     d_recv,
 ):
@@ -149,6 +150,8 @@
     at_end = jnp.where(place == ZN - 1, 1, 0)
     before = flip(lax.rem(work + n_dom - at_start, n_dom))
     beyond = flip(lax.rem(work + at_end, n_dom))
+    before_block = lax.rem(work + n_dom - 1, n_dom)
+    after_block = lax.rem(work + 1, n_dom)
     below = (body * ZN + lax.rem(place + ZN - 1, ZN), before)
     above = (body * ZN + lax.rem(place + 1, ZN), beyond)
 
@@ -165,6 +168,17 @@
         pl.semaphore_signal(barrier, inc=1, device_id=(j, work), device_id_type=MESH)
     for device in ((inst, left), (inst, right), below, above):
         pl.semaphore_signal(barrier, inc=1, device_id=device, device_id_type=MESH)
+
+    core = lax.rem(dom, 2)
+    gets_handed = [body * core, (1 - body) * (1 - core)]
+    hands_on = [body * (1 - core), (1 - body) * core]
+    for side, block in ((0, right), (1, left)):
+
+        @pl.when(gets_handed[side] == 1)
+        def _(side=side, block=block):
+            for q in range(ZN):
+                device = ((1 - side) * ZN + q, flip(block))
+                pl.semaphore_signal(barrier, inc=1, device_id=device, device_id_type=MESH)
 
     def remote(source, target, send, recv, device):
         return pltpu.make_async_remote_copy(
@@ -336,19 +350,48 @@
         for v in range(NV):
             win[it, 0, v, 0:T] = cur[v, 2]
             win[it, 1, v, T : 2 * T] = cur[v, 1]
-        return start(
-            [
-                near(10 * it + 2, win.at[it, 0, :, 0:T], win.at[it, 0, :, T : 2 * T], left),
-                near(10 * it + 3, win.at[it, 1, :, T : 2 * T], win.at[it, 1, :, 0:T], right),
-            ]
-        )
+        windows = [
+            near(10 * it + 2, win.at[it, 0, :, 0:T], win.at[it, 0, :, T : 2 * T], left),
+            near(10 * it + 3, win.at[it, 1, :, T : 2 * T], win.at[it, 1, :, 0:T], right),
+        ]
+        if it > 0:
+            return start(windows)
+        for side in range(2):
+            pl.when(hands_on[side] == 0)(windows[side].start)
+        return windows
+
+    def hand_on():
+        for side, block in ((0, before_block), (1, after_block)):
+            rows = pl.ds(pl.multiple_of((1 - side) * T + SLAB * place, SLAB), SLAB)
+
+            @pl.when(hands_on[side] == 1)
+            def _(side=side, block=block, rows=rows):
+                for n in range(ZN):
+                    m = (1 - side) * ZN + lax.rem(place + n, ZN)
+                    remote(
+                        in_u.at[0, m],
+                        win.at[0, side, :, rows],
+                        f_send,
+                        d_recv.at[2 + side],
+                        (m, block),
+                    ).start()
+
+    def handed_on():
+        for side in range(2):
+
+            @pl.when(hands_on[side] == 1)
+            def _():
+                ref = in_u.at[0, 0:ZN]
+                pltpu.make_async_copy(ref, ref, f_send).wait()
+
+            pl.when(hands_on[side] == 0)(windows[side].wait_send)
 
     def rim_of(slot, out, back, spots):
         return start(both(slot, lambda side: out.at[side, spots], lambda side: back.at[side, spots]))
 
     FRONT, REST = pl.ds(0, 2), pl.ds(2, 2)
 
-    pl.semaphore_wait(barrier, NI + 4)
+    pl.semaphore_wait(barrier, NI + 4 + ZN * (hands_on[0] + hands_on[1]))
     for part in range(2):
         send(0, part)
     for c in loads:
@@ -386,6 +429,7 @@
     half = T // 16
     inside(n0, 0, half)
     arrive(0, 0)
+    hand_on()
     spectral(0, w1)
     send(1, 0)
     arrive(0, 1)
@@ -490,8 +534,9 @@
         c.wait()
     put_rows(rhalo, (0, 1))
     gone(0)
-    for c in layers + windows:
+    for c in layers:
         c.wait_send()
+    handed_on()
     first_update((0, 1))
     windows = interface_rows(1)
     send(3, 1)
@@ -612,6 +657,7 @@
             pltpu.SemaphoreType.DMA((5,)),
             pltpu.SemaphoreType.DMA((4,)),
             pltpu.SemaphoreType.DMA((4, 2)),
+            pltpu.SemaphoreType.DMA,
             pltpu.SemaphoreType.DMA((22,)),
             pltpu.SemaphoreType.DMA((22,)),
         ],

time: 58.5 us -> 59.8 us (1.022)
  Pallas kernels: 54.6 us -> 55.9 us
    pallas_call x1, Pallas kernels: 54.6 us -> 55.9 us  [local(): pl.pallas_call(functools.partial(kernel, n_dom, n_dom * T), out_shape=[ja...]
where the time goes in v6:
time: 59.8 us; the launch traced here: 59.6 us
  Pallas kernels  55.9 us (93%)
  local copies, waits for them, and re-layouts  2.44 us (4%)
  between operations  1.3 us (2%)
    pallas_call x1, Pallas kernels, local(): pl.pallas_call(functools.partial(kernel, n_dom, n_dom * T), out_shape=[ja...  55.9 us
    unnamed x6, local copies, waits for them, and re-layouts  2.44 us

profile of v6, /device:TPU:0, one launch (start us, length us, event | category | flops | bytes accessed | tf_op | source)
XLA Modules:
  0.0 59.6 jit_solution(8907363576445264006)
XLA Ops:
  1.3 0.0 copy-start.1
  1.3 0.0 copy-start
  1.3 0.7 %copy-done.1 = f32[1,2,64]{2,1,0:T(2,128)S(1)} copy-done((f32[1,2,64]{2,1,0:T(2,128)S(1)}, f32[1,2,64]{2,1,0:T(2,128)}, u32[]{:S(2)}) %copy-start.1) | copy-done | bytes 536
  2.0 0.0 copy-done
  2.0 55.9 %shard_map.59 = (f32[6,4,64,128]{3,2,1,0:T(8,128)S(1)}, f32[6,4,64,128]{3,2,1,0:T(8,128)S(1)}) custom-call(f32[6,4,64,128]{3,2,1,0:T(8,128)} %bitcast.9, s32[2,64]{1,0:T(2,128)S(1)} %bitcast.7, f32[2,64]{1,0:T(2,128)S(1)} %bitcast.8, s32[1]{0:T(128)S(6)} %copy.8.count), custom_call_target="tpu_custom_call" | custom-call | flops 20000000 | bytes 2359296 | tf_op jit(solution)/shard_map/pallas_call | solution.py:620
  57.9 0.9 %copy.9 = f32[1,6,4,64,128]{4,3,2,1,0:T(8,128)} copy(f32[1,6,4,64,128]{4,3,2,1,0:T(8,128)S(1)} %bitcast.6) | data formatting | bytes 1572864
  58.7 0.9 %copy.10 = f32[1,6,4,64,128]{4,3,2,1,0:T(8,128)} copy(f32[1,6,4,64,128]{4,3,2,1,0:T(8,128)S(1)} %bitcast.5) | data formatting | bytes 1572864
Async XLA Ops:
  1.3 0.7 %copy-start.1 = (f32[1,2,64]{2,1,0:T(2,128)S(1)}, f32[1,2,64]{2,1,0:T(2,128)}, u32[]{:S(2)}) copy-start(f32[1,2,64]{2,1,0:T(2,128)} %param.6) | copy-start | bytes 1540
  1.3 0.7 %copy-start = (s32[1,2,64]{2,1,0:T(2,128)S(1)}, s32[1,2,64]{2,1,0:T(2,128)}, u32[]{:S(2)}) copy-start(s32[1,2,64]{2,1,0:T(2,128)} %param.5) | copy-start | bytes 1540

commit v7 on v5

--- a/solution.py
+++ b/solution.py
@@ -129,9 +129,12 @@
     slab_b,
     slab_out,
     slab_in,
+    relay,
     load_sem,
     p_send,
     p_recv,
+    r_send,
+    r_recv,
     d_send,
     d_recv,
 ):
@@ -163,7 +166,8 @@
     barrier = pltpu.get_barrier_semaphore()
     for j in range(NI):
         pl.semaphore_signal(barrier, inc=1, device_id=(j, work), device_id_type=MESH)
-    for device in ((inst, left), (inst, right), below, above):
+    ring = [(body * ZN + lax.rem(place + dz, ZN), dom) for dz in (1, ZN - 1)]
+    for device in ((inst, left), (inst, right), below, above, ring[0], ring[1]):
         pl.semaphore_signal(barrier, inc=1, device_id=device, device_id_type=MESH)
 
     def remote(source, target, send, recv, device):
@@ -176,29 +180,62 @@
             device_id_type=MESH,
         )
 
-    def piece(unit, partner, part, slot):
+    def source_of(unit, partner, part):
         side, slab = partner // ZN, lax.rem(partner, ZN)
         row = 1 + side if part == 0 else (AX - 1) * side
         mine = pl.ds(pl.multiple_of(SLAB * slab, SLAB), SLAB)
+        if unit == 0:
+            return flow.at[:, row, mine]
+        if unit == 2:
+            return n0.at[:, row, mine]
+        return (w1 if unit == 1 else w2).at[part, partner]
+
+    def target_of(unit, part, slot):
         spot = 2 * part + slot // ZN
         at = SLAB * lax.rem(slot, ZN)
         if unit == 0:
-            source, target = flow.at[:, row, mine], in_u.at[part, slot]
-        elif unit == 1:
-            source = w1.at[part, partner]
-            target = ss.at[spot, :, pl.ds(pl.multiple_of(at, SLAB), SLAB)]
-        elif unit == 2:
-            source, target = n0.at[:, row, mine], in_n.at[slot]
-        else:
-            source = w2.at[part, partner]
-            target = ww.at[spot, :, pl.ds(pl.multiple_of(at + 8, 8), SLAB)]
-        return remote(source, target, p_send.at[unit], p_recv.at[unit, part], (partner, work))
+            return in_u.at[part, slot]
+        if unit == 1:
+            return ss.at[spot, :, pl.ds(pl.multiple_of(at, SLAB), SLAB)]
+        if unit == 2:
+            return in_n.at[slot]
+        return ww.at[spot, :, pl.ds(pl.multiple_of(at + 8, 8), SLAB)]
 
     order = [lax.rem(inst + n, NI) for n in range(NI)]
+    ahead, behind = lax.rem(place + 1, ZN), lax.rem(place + ZN - 1, ZN)
 
     def send(unit, part):
-        for j in order:
-            piece(unit, j, part, inst).start()
+        for way, n in enumerate((2, 6)):
+            via = order[n] // ZN * ZN + (ahead, behind)[way]
+            remote(
+                source_of(unit, order[n], part),
+                relay.at[unit, part, way],
+                p_send.at[unit],
+                r_recv.at[unit, part, way],
+                (via, work),
+            ).start()
+        for n in (0, 1, 3, 4, 5, 7):
+            remote(
+                source_of(unit, order[n], part),
+                target_of(unit, part, inst),
+                p_send.at[unit],
+                p_recv.at[unit, part],
+                (order[n], work),
+            ).start()
+
+    def hand_on(unit, part):
+        for way, (sender, onward) in enumerate(((behind, ahead), (ahead, behind))):
+            wraps = jnp.where(sender >= 2, 1, 0)
+            origin = lax.rem(body + wraps + way, 2) * ZN + sender
+            held = relay.at[unit, part, way]
+            pltpu.make_async_copy(held, held, r_recv.at[unit, part, way]).wait()
+            remote(
+                held,
+                target_of(unit, part, origin),
+                r_send.at[unit],
+                p_recv.at[unit, part],
+                (body * ZN + onward, dom),
+            ).start()
 
     def arrive(unit, part):
         spots = pl.ds(2 * part, 2)
@@ -208,6 +245,8 @@
     def gone(unit):
         ref = (flow, w1, n0.at[:, 1:3], w2)[unit]
         pltpu.make_async_copy(ref, ref, p_send.at[unit]).wait()
+        ref = relay.at[2, 0] if unit == 2 else relay.at[unit]
+        pltpu.make_async_copy(ref, ref, r_send.at[unit]).wait()
 
     def near(slot, source, target, device):
         return remote(source, target, d_send.at[slot], d_recv.at[slot], (inst, device))
@@ -348,7 +387,7 @@
 
     FRONT, REST = pl.ds(0, 2), pl.ds(2, 2)
 
-    pl.semaphore_wait(barrier, NI + 4)
+    pl.semaphore_wait(barrier, NI + 6)
     for part in range(2):
         send(0, part)
     for c in loads:
@@ -384,7 +423,9 @@
             coef[side, i] = jnp.broadcast_to(column, (T, S))
 
     half = T // 16
+    hand_on(0, 0)
     inside(n0, 0, half)
+    hand_on(0, 1)
     arrive(0, 0)
     spectral(0, w1)
     send(1, 0)
@@ -400,8 +441,10 @@
     )
     spectral(1, w1)
     send(1, 1)
+    hand_on(1, 0)
     inside(n0, half, 2 * half)
     around(n0, 0, layers)
+    hand_on(1, 1)
     interface(n0, 0, windows)
     send(2, 0)
 
@@ -426,6 +469,7 @@
                 slab_n[m, v, rows, :] = r[v] + (toward * (f1[v] - f[v]) - (c1[v] + c[v]))
 
     over(NI, slab_inside)
+    hand_on(2, 0)
     for c in slabs:
         c.wait()
     low = prev_terms([slab_in[0, v] for v in range(NV)], 1)
@@ -501,11 +545,14 @@
     put_rows(rhalo, (2, 3))
     first_update((2, 3))
     layers = outer_layers(1)
+    hand_on(3, 1)
 
     arrive(2, 0)
     spectral(0, w2, lambda m, v, t0: in_n[m, v, t0 : t0 + 8, :])
     send(3, 0)
-    inside(n1, 0, 2 * half)
+    inside(n1, 0, half)
+    hand_on(3, 0)
+    inside(n1, half, 2 * half)
     around(n1, 1, layers)
 
     def second_sum(spot, v, t0, t1):
@@ -609,9 +656,12 @@
             pltpu.VMEM((NI, NV, SLAB + 8, S), f32),
             pltpu.VMEM((2, NV, NI, S), f32),
             pltpu.VMEM((2, NV, NI, S), f32),
+            pltpu.VMEM((4, 2, 2, NV, SLAB, S), f32),
             pltpu.SemaphoreType.DMA((5,)),
             pltpu.SemaphoreType.DMA((4,)),
             pltpu.SemaphoreType.DMA((4, 2)),
+            pltpu.SemaphoreType.DMA((4,)),
+            pltpu.SemaphoreType.DMA((4, 2, 2)),
             pltpu.SemaphoreType.DMA((22,)),
             pltpu.SemaphoreType.DMA((22,)),
         ],

time: 58.5 us -> 61.1 us (1.044); the launches traced: 58.3 us -> 59.9 us
  Pallas kernels: 54.6 us -> 56.2 us
    pallas_call x1, Pallas kernels: 54.6 us -> 56.2 us  [local(): pl.pallas_call(functools.partial(kernel, n_dom, n_dom * T), out_shape=[ja...]
where the time goes in v7:
time: 61.1 us; the launch traced here: 59.9 us
  Pallas kernels  56.2 us (92%)
  local copies, waits for them, and re-layouts  2.44 us (4%)
  between operations  1.3 us (2%)
    pallas_call x1, Pallas kernels, local(): pl.pallas_call(functools.partial(kernel, n_dom, n_dom * T), out_shape=[ja...  56.2 us
    unnamed x6, local copies, waits for them, and re-layouts  2.44 us

profile of v7, /device:TPU:0, one launch (start us, length us, event | category | flops | bytes accessed | tf_op | source)
XLA Modules:
  0.0 59.9 jit_solution(735499317001989231)
XLA Ops:
  1.3 0.0 copy-start.1
  1.3 0.0 copy-start
  1.3 0.7 %copy-done.1 = f32[1,2,64]{2,1,0:T(2,128)S(1)} copy-done((f32[1,2,64]{2,1,0:T(2,128)S(1)}, f32[1,2,64]{2,1,0:T(2,128)}, u32[]{:S(2)}) %copy-start.1) | copy-done | bytes 536
  2.0 0.0 copy-done
  2.0 56.2 %shard_map.59 = (f32[6,4,64,128]{3,2,1,0:T(8,128)S(1)}, f32[6,4,64,128]{3,2,1,0:T(8,128)S(1)}) custom-call(f32[6,4,64,128]{3,2,1,0:T(8,128)} %bitcast.9, s32[2,64]{1,0:T(2,128)S(1)} %bitcast.7, f32[2,64]{1,0:T(2,128)S(1)} %bitcast.8, s32[1]{0:T(128)S(6)} %copy.8.count), custom_call_target="tpu_custom_call" | custom-call | flops 20000000 | bytes 2359296 | tf_op jit(solution)/shard_map/pallas_call | solution.py:622
  58.2 0.9 %copy.9 = f32[1,6,4,64,128]{4,3,2,1,0:T(8,128)} copy(f32[1,6,4,64,128]{4,3,2,1,0:T(8,128)S(1)} %bitcast.6) | data formatting | bytes 1572864
  59.1 0.9 %copy.10 = f32[1,6,4,64,128]{4,3,2,1,0:T(8,128)} copy(f32[1,6,4,64,128]{4,3,2,1,0:T(8,128)S(1)} %bitcast.5) | data formatting | bytes 1572864
Async XLA Ops:
  1.3 0.7 %copy-start.1 = (f32[1,2,64]{2,1,0:T(2,128)S(1)}, f32[1,2,64]{2,1,0:T(2,128)}, u32[]{:S(2)}) copy-start(f32[1,2,64]{2,1,0:T(2,128)} %param.6) | copy-start | bytes 1540
  1.3 0.7 %copy-start = (s32[1,2,64]{2,1,0:T(2,128)S(1)}, s32[1,2,64]{2,1,0:T(2,128)}, u32[]{:S(2)}) copy-start(s32[1,2,64]{2,1,0:T(2,128)} %param.5) | copy-start | bytes 1540

commit v8 on v4

--- a/solution.py
+++ b/solution.py
@@ -303,11 +303,9 @@
 
         over(NV, variable)
 
-    def interface(out, it, windows):
-        for c in windows:
-            c.wait_recv()
-
-        def ghosts(i):
+    def interface(out, it, tiles):
+        def ghosts(n):
+            i = tiles[0] + n * tiles[2]
             t0 = pl.multiple_of(8 * i, 8)
             for side in range(2):
                 taps = [coef[side, n, pl.ds(t0, 8), :] for n in range(3)]
@@ -321,7 +319,7 @@
                 for v in range(NV):
                     out[v, 1 + side, pl.ds(t0, 8), :] += terms[v]
 
-        over(T // 8, ghosts)
+        over(tiles[1], ghosts)
 
     def outer_layers(it):
         for side, t in enumerate((0, T - 1)):
@@ -386,11 +384,13 @@
             coef[side, i] = jnp.broadcast_to(column, (T, S))
 
     half = T // 16
-    inside(n0, 0, half)
     arrive(0, 0)
     spectral(0, w1)
     send(1, 0)
+    inside(n0, 0, half)
     arrive(0, 1)
+    spectral(1, w1)
+    send(1, 1)
     for v in range(NV):
         slab_out[0, v] = in_u[1, :, v, 0, :]
         slab_out[1, v] = in_u[1, :, v, SLAB - 1, :]
@@ -400,11 +400,11 @@
             remote(slab_out.at[1], slab_in.at[0], d_send.at[19], d_recv.at[19], above),
         ]
     )
-    spectral(1, w1)
-    send(1, 1)
     inside(n0, half, 2 * half)
     around(n0, 0, layers)
-    interface(n0, 0, windows)
+    for c in windows:
+        c.wait_recv()
+    interface(n0, 0, (0, T // 8, 1))
     send(2, 0)
 
     toward = jnp.where(body == 0, 1.0, -1.0)
@@ -515,9 +515,12 @@
 
     keep_rows(qedge, (2, 3), ends, second_sum)
     rim2 = rim_of(8, qedge, qhalo, REST)
-    interface(n1, 1, windows)
+    for c in windows:
+        c.wait_recv()
+    interface(n1, 1, (0, 2, T // 8 - 1))
     keep_rows(qedge, (0, 1), ends, second_sum)
     rim = rim_of(12 + 2, qedge, qhalo, FRONT)
+    interface(n1, 1, (1, T // 8 - 2, 1))
 
     far_rows = (0, 1, 2, 3, T - 4, T - 3, T - 2, T - 1)
 

time: 58.5 us -> 58.4 us (level)
  no operation moved by 1% of the time
where the time goes in v8:
time: 58.4 us; the launch traced here: 58.3 us
  Pallas kernels  54.6 us (93%)
  local copies, waits for them, and re-layouts  2.44 us (4%)
  between operations  1.3 us (2%)
    pallas_call x1, Pallas kernels, local(): pl.pallas_call(functools.partial(kernel, n_dom, n_dom * T), out_shape=[ja...  54.6 us
    unnamed x6, local copies, waits for them, and re-layouts  2.44 us

profile of v8, /device:TPU:0, one launch (start us, length us, event | category | flops | bytes accessed | tf_op | source)
XLA Modules:
  0.0 58.3 jit_solution(3849390705049207076)
XLA Ops:
  1.3 0.0 copy-start.1
  1.3 0.0 copy-start
  1.3 0.7 %copy-done.1 = f32[1,2,64]{2,1,0:T(2,128)S(1)} copy-done((f32[1,2,64]{2,1,0:T(2,128)S(1)}, f32[1,2,64]{2,1,0:T(2,128)}, u32[]{:S(2)}) %copy-start.1) | copy-done | bytes 536
  2.0 0.0 copy-done
  2.0 54.6 %shard_map.59 = (f32[6,4,64,128]{3,2,1,0:T(8,128)S(1)}, f32[6,4,64,128]{3,2,1,0:T(8,128)S(1)}) custom-call(f32[6,4,64,128]{3,2,1,0:T(8,128)} %bitcast.9, s32[2,64]{1,0:T(2,128)S(1)} %bitcast.7, f32[2,64]{1,0:T(2,128)S(1)} %bitcast.8, s32[1]{0:T(128)S(6)} %copy.8.count), custom_call_target="tpu_custom_call" | custom-call | flops 20000000 | bytes 2359296 | tf_op jit(solution)/shard_map/pallas_call | solution.py:586
  56.5 0.9 %copy.9 = f32[1,6,4,64,128]{4,3,2,1,0:T(8,128)} copy(f32[1,6,4,64,128]{4,3,2,1,0:T(8,128)S(1)} %bitcast.6) | data formatting | bytes 1572864
  57.4 0.9 %copy.10 = f32[1,6,4,64,128]{4,3,2,1,0:T(8,128)} copy(f32[1,6,4,64,128]{4,3,2,1,0:T(8,128)S(1)} %bitcast.5) | data formatting | bytes 1572864
Async XLA Ops:
  1.3 0.7 %copy-start.1 = (f32[1,2,64]{2,1,0:T(2,128)S(1)}, f32[1,2,64]{2,1,0:T(2,128)}, u32[]{:S(2)}) copy-start(f32[1,2,64]{2,1,0:T(2,128)} %param.6) | copy-start | bytes 1540
  1.3 0.7 %copy-start = (s32[1,2,64]{2,1,0:T(2,128)S(1)}, s32[1,2,64]{2,1,0:T(2,128)}, u32[]{:S(2)}) copy-start(s32[1,2,64]{2,1,0:T(2,128)} %param.5) | copy-start | bytes 1540

commit v9 on v8

--- a/solution.py
+++ b/solution.py
@@ -140,15 +140,12 @@
     left = lax.rem(dom + n_dom - 1, n_dom)
     right = lax.rem(dom + 1, n_dom)
 
-    def flip(d):
-        return d + 2 - 4 * lax.rem(d // 2, 2)
-
-    work = flip(dom)
+    others = [lax.rem(inst + n, NI) for n in range(1, NI)]
     body, place = inst // ZN, lax.rem(inst, ZN)
     at_start = jnp.where(place == 0, 1, 0)
     at_end = jnp.where(place == ZN - 1, 1, 0)
-    before = flip(lax.rem(work + n_dom - at_start, n_dom))
-    beyond = flip(lax.rem(work + at_end, n_dom))
+    before = lax.rem(dom + n_dom - at_start, n_dom)
+    beyond = lax.rem(dom + at_end, n_dom)
     below = (body * ZN + lax.rem(place + ZN - 1, ZN), before)
     above = (body * ZN + lax.rem(place + 1, ZN), beyond)
 
@@ -161,8 +158,8 @@
     for c in loads:
         c.start()
     barrier = pltpu.get_barrier_semaphore()
-    for j in range(NI):
-        pl.semaphore_signal(barrier, inc=1, device_id=(j, work), device_id_type=MESH)
+    for j in others:
+        pl.semaphore_signal(barrier, inc=1, device_id=(j, dom), device_id_type=MESH)
     for device in ((inst, left), (inst, right), below, above):
         pl.semaphore_signal(barrier, inc=1, device_id=device, device_id_type=MESH)
 
@@ -176,29 +173,34 @@
             device_id_type=MESH,
         )
 
-    def piece(unit, partner, part, slot):
+    def source_of(unit, partner, part):
         side, slab = partner // ZN, lax.rem(partner, ZN)
         row = 1 + side if part == 0 else (AX - 1) * side
         mine = pl.ds(pl.multiple_of(SLAB * slab, SLAB), SLAB)
+        if unit == 0:
+            return flow.at[:, row, mine]
+        if unit == 2:
+            return n0.at[:, row, mine]
+        return (w1 if unit == 1 else w2).at[part, partner]
+
+    def target_of(unit, part, slot):
         spot = 2 * part + slot // ZN
         at = SLAB * lax.rem(slot, ZN)
         if unit == 0:
-            source, target = flow.at[:, row, mine], in_u.at[part, slot]
-        elif unit == 1:
-            source = w1.at[part, partner]
-            target = ss.at[spot, :, pl.ds(pl.multiple_of(at, SLAB), SLAB)]
-        elif unit == 2:
-            source, target = n0.at[:, row, mine], in_n.at[slot]
-        else:
-            source = w2.at[part, partner]
-            target = ww.at[spot, :, pl.ds(pl.multiple_of(at + 8, 8), SLAB)]
-        return remote(source, target, p_send.at[unit], p_recv.at[unit, part], (partner, work))
-
-    order = [lax.rem(inst + n, NI) for n in range(NI)]
+            return in_u.at[part, slot]
+        if unit == 1:
+            return ss.at[spot, :, pl.ds(pl.multiple_of(at, SLAB), SLAB)]
+        if unit == 2:
+            return in_n.at[slot]
+        return ww.at[spot, :, pl.ds(pl.multiple_of(at + 8, 8), SLAB)]
 
     def send(unit, part):
-        for j in order:
-            piece(unit, j, part, inst).start()
+        target = target_of(unit, part, inst)
+        for j in others:
+            remote(
+                source_of(unit, j, part), target, p_send.at[unit], p_recv.at[unit, part], (j, dom)
+            ).start()
+        pltpu.make_async_copy(source_of(unit, inst, part), target, p_recv.at[unit, part]).start()
 
     def arrive(unit, part):
         spots = pl.ds(2 * part, 2)
@@ -206,7 +208,7 @@
         pltpu.make_async_copy(ref, ref, p_recv.at[unit, part]).wait()
 
     def gone(unit):
-        ref = (flow, w1, n0.at[:, 1:3], w2)[unit]
+        ref = in_n.at[0 : NI - 1] if unit == 2 else w1.at[:, 0 : NI - 1]
         pltpu.make_async_copy(ref, ref, p_send.at[unit]).wait()
 
     def near(slot, source, target, device):
@@ -348,7 +350,7 @@
 
     FRONT, REST = pl.ds(0, 2), pl.ds(2, 2)
 
-    pl.semaphore_wait(barrier, NI + 4)
+    pl.semaphore_wait(barrier, NI + 3)
     for part in range(2):
         send(0, part)
     for c in loads:

time: 58.4 us -> 57.5 us (0.985)
  Pallas kernels: 54.6 us -> 53.6 us
    pallas_call x1, Pallas kernels: 54.6 us -> 53.6 us  [local(): pl.pallas_call(functools.partial(kernel, n_dom, n_dom * T), out_shape=[ja...]
where the time goes in v9:
time: 57.5 us; the launch traced here: 57.3 us
  Pallas kernels  53.6 us (93%)
  local copies, waits for them, and re-layouts  2.44 us (4%)
  between operations  1.3 us (2%)
    pallas_call x1, Pallas kernels, local(): pl.pallas_call(functools.partial(kernel, n_dom, n_dom * T), out_shape=[ja...  53.6 us
    unnamed x6, local copies, waits for them, and re-layouts  2.44 us

profile of v9, /device:TPU:0, one launch (start us, length us, event | category | flops | bytes accessed | tf_op | source)
XLA Modules:
  0.0 57.3 jit_solution(4062990204911750186)
XLA Ops:
  1.3 0.0 copy-start.1
  1.3 0.0 copy-start
  1.3 0.7 %copy-done.1 = f32[1,2,64]{2,1,0:T(2,128)S(1)} copy-done((f32[1,2,64]{2,1,0:T(2,128)S(1)}, f32[1,2,64]{2,1,0:T(2,128)}, u32[]{:S(2)}) %copy-start.1) | copy-done | bytes 536
  2.0 0.0 copy-done
  2.0 53.6 %shard_map.59 = (f32[6,4,64,128]{3,2,1,0:T(8,128)S(1)}, f32[6,4,64,128]{3,2,1,0:T(8,128)S(1)}) custom-call(f32[6,4,64,128]{3,2,1,0:T(8,128)} %bitcast.9, s32[2,64]{1,0:T(2,128)S(1)} %bitcast.7, f32[2,64]{1,0:T(2,128)S(1)} %bitcast.8, s32[1]{0:T(128)S(6)} %copy.8.count), custom_call_target="tpu_custom_call" | custom-call | flops 20000000 | bytes 2359296 | tf_op jit(solution)/shard_map/pallas_call | solution.py:588
  55.5 0.9 %copy.9 = f32[1,6,4,64,128]{4,3,2,1,0:T(8,128)} copy(f32[1,6,4,64,128]{4,3,2,1,0:T(8,128)S(1)} %bitcast.6) | data formatting | bytes 1572864
  56.4 0.9 %copy.10 = f32[1,6,4,64,128]{4,3,2,1,0:T(8,128)} copy(f32[1,6,4,64,128]{4,3,2,1,0:T(8,128)S(1)} %bitcast.5) | data formatting | bytes 1572864
Async XLA Ops:
  1.3 0.7 %copy-start.1 = (f32[1,2,64]{2,1,0:T(2,128)S(1)}, f32[1,2,64]{2,1,0:T(2,128)}, u32[]{:S(2)}) copy-start(f32[1,2,64]{2,1,0:T(2,128)} %param.6) | copy-start | bytes 1540
  1.3 0.7 %copy-start = (s32[1,2,64]{2,1,0:T(2,128)S(1)}, s32[1,2,64]{2,1,0:T(2,128)}, u32[]{:S(2)}) copy-start(s32[1,2,64]{2,1,0:T(2,128)} %param.5) | copy-start | bytes 1540

commit v10 on v5

--- a/solution.py
+++ b/solution.py
@@ -140,15 +140,17 @@
     left = lax.rem(dom + n_dom - 1, n_dom)
     right = lax.rem(dom + 1, n_dom)
 
-    def flip(d):
-        return d + 2 - 4 * lax.rem(d // 2, 2)
-
-    work = flip(dom)
     body, place = inst // ZN, lax.rem(inst, ZN)
+    others = [
+        lax.rem(body + other, 2) * ZN + lax.rem(place + dz, ZN)
+        for other in (1, 0)
+        for dz in (2, 1, 3, 0)
+        if other or dz
+    ]
     at_start = jnp.where(place == 0, 1, 0)
     at_end = jnp.where(place == ZN - 1, 1, 0)
-    before = flip(lax.rem(work + n_dom - at_start, n_dom))
-    beyond = flip(lax.rem(work + at_end, n_dom))
+    before = lax.rem(dom + n_dom - at_start, n_dom)
+    beyond = lax.rem(dom + at_end, n_dom)
     below = (body * ZN + lax.rem(place + ZN - 1, ZN), before)
     above = (body * ZN + lax.rem(place + 1, ZN), beyond)
 
@@ -161,8 +163,8 @@
     for c in loads:
         c.start()
     barrier = pltpu.get_barrier_semaphore()
-    for j in range(NI):
-        pl.semaphore_signal(barrier, inc=1, device_id=(j, work), device_id_type=MESH)
+    for j in others:
+        pl.semaphore_signal(barrier, inc=1, device_id=(j, dom), device_id_type=MESH)
     for device in ((inst, left), (inst, right), below, above):
         pl.semaphore_signal(barrier, inc=1, device_id=device, device_id_type=MESH)
 
@@ -176,29 +178,34 @@
             device_id_type=MESH,
         )
 
-    def piece(unit, partner, part, slot):
+    def source_of(unit, partner, part):
         side, slab = partner // ZN, lax.rem(partner, ZN)
         row = 1 + side if part == 0 else (AX - 1) * side
         mine = pl.ds(pl.multiple_of(SLAB * slab, SLAB), SLAB)
+        if unit == 0:
+            return flow.at[:, row, mine]
+        if unit == 2:
+            return n0.at[:, row, mine]
+        return (w1 if unit == 1 else w2).at[part, partner]
+
+    def target_of(unit, part, slot):
         spot = 2 * part + slot // ZN
         at = SLAB * lax.rem(slot, ZN)
         if unit == 0:
-            source, target = flow.at[:, row, mine], in_u.at[part, slot]
-        elif unit == 1:
-            source = w1.at[part, partner]
-            target = ss.at[spot, :, pl.ds(pl.multiple_of(at, SLAB), SLAB)]
-        elif unit == 2:
-            source, target = n0.at[:, row, mine], in_n.at[slot]
-        else:
-            source = w2.at[part, partner]
-            target = ww.at[spot, :, pl.ds(pl.multiple_of(at + 8, 8), SLAB)]
-        return remote(source, target, p_send.at[unit], p_recv.at[unit, part], (partner, work))
-
-    order = [lax.rem(inst + n, NI) for n in range(NI)]
+            return in_u.at[part, slot]
+        if unit == 1:
+            return ss.at[spot, :, pl.ds(pl.multiple_of(at, SLAB), SLAB)]
+        if unit == 2:
+            return in_n.at[slot]
+        return ww.at[spot, :, pl.ds(pl.multiple_of(at + 8, 8), SLAB)]
 
     def send(unit, part):
-        for j in order:
-            piece(unit, j, part, inst).start()
+        target = target_of(unit, part, inst)
+        for j in others:
+            remote(
+                source_of(unit, j, part), target, p_send.at[unit], p_recv.at[unit, part], (j, dom)
+            ).start()
+        pltpu.make_async_copy(source_of(unit, inst, part), target, p_recv.at[unit, part]).start()
 
     def arrive(unit, part):
         spots = pl.ds(2 * part, 2)
@@ -206,7 +213,7 @@
         pltpu.make_async_copy(ref, ref, p_recv.at[unit, part]).wait()
 
     def gone(unit):
-        ref = (flow, w1, n0.at[:, 1:3], w2)[unit]
+        ref = in_n.at[0 : NI - 1] if unit == 2 else w1.at[:, 0 : NI - 1]
         pltpu.make_async_copy(ref, ref, p_send.at[unit]).wait()
 
     def near(slot, source, target, device):
@@ -303,11 +310,9 @@
 
         over(NV, variable)
 
-    def interface(out, it, windows):
-        for c in windows:
-            c.wait_recv()
-
-        def ghosts(i):
+    def interface(out, it, tiles):
+        def ghosts(n):
+            i = tiles[0] + n * tiles[2]
             t0 = pl.multiple_of(8 * i, 8)
             for side in range(2):
                 taps = [coef[side, n, pl.ds(t0, 8), :] for n in range(3)]
@@ -321,7 +326,7 @@
                 for v in range(NV):
                     out[v, 1 + side, pl.ds(t0, 8), :] += terms[v]
 
-        over(T // 8, ghosts)
+        over(tiles[1], ghosts)
 
     def outer_layers(it):
         for side, t in enumerate((0, T - 1)):
@@ -348,7 +353,7 @@
 
     FRONT, REST = pl.ds(0, 2), pl.ds(2, 2)
 
-    pl.semaphore_wait(barrier, NI + 4)
+    pl.semaphore_wait(barrier, NI + 3)
     for part in range(2):
         send(0, part)
     for c in loads:
@@ -384,11 +389,13 @@
             coef[side, i] = jnp.broadcast_to(column, (T, S))
 
     half = T // 16
-    inside(n0, 0, half)
     arrive(0, 0)
     spectral(0, w1)
     send(1, 0)
+    inside(n0, 0, half)
     arrive(0, 1)
+    spectral(1, w1)
+    send(1, 1)
     for v in range(NV):
         slab_out[0, v] = in_u[1, :, v, 0, :]
         slab_out[1, v] = in_u[1, :, v, SLAB - 1, :]
@@ -398,11 +405,11 @@
             remote(slab_out.at[1], slab_in.at[0], d_send.at[19], d_recv.at[19], above),
         ]
     )
-    spectral(1, w1)
-    send(1, 1)
     inside(n0, half, 2 * half)
     around(n0, 0, layers)
-    interface(n0, 0, windows)
+    for c in windows:
+        c.wait_recv()
+    interface(n0, 0, (0, T // 8, 1))
     send(2, 0)
 
     toward = jnp.where(body == 0, 1.0, -1.0)
@@ -513,9 +520,12 @@
 
     keep_rows(qedge, (2, 3), second_sum)
     rim2 = rim_of(8, qedge, qhalo, REST)
-    interface(n1, 1, windows)
+    for c in windows:
+        c.wait_recv()
+    interface(n1, 1, (0, 2, T // 8 - 1))
     keep_rows(qedge, (0, 1), second_sum)
     rim = rim_of(12 + 2, qedge, qhalo, FRONT)
+    interface(n1, 1, (1, T // 8 - 2, 1))
 
     def last_source(spot, v, t0, t1):
         return ww[spot, v, 8 + t0 : 8 + t1, :]

time: 58.5 us -> 58.3 us (level)
  no operation moved by 1% of the time
where the time goes in v10:
time: 58.3 us; the launch traced here: 58.1 us
  Pallas kernels  54.4 us (93%)
  local copies, waits for them, and re-layouts  2.44 us (4%)
  between operations  1.3 us (2%)
    pallas_call x1, Pallas kernels, local(): pl.pallas_call(functools.partial(kernel, n_dom, n_dom * T), out_shape=[ja...  54.4 us
    unnamed x6, local copies, waits for them, and re-layouts  2.44 us

profile of v10, /device:TPU:0, one launch (start us, length us, event | category | flops | bytes accessed | tf_op | source)
XLA Modules:
  0.0 58.1 jit_solution(16395564882991105659)
XLA Ops:
  1.3 0.0 copy-start.1
  1.3 0.0 copy-start
  1.3 0.7 %copy-done.1 = f32[1,2,64]{2,1,0:T(2,128)S(1)} copy-done((f32[1,2,64]{2,1,0:T(2,128)S(1)}, f32[1,2,64]{2,1,0:T(2,128)}, u32[]{:S(2)}) %copy-start.1) | copy-done | bytes 536
  2.0 0.0 copy-done
  2.0 54.4 %shard_map.59 = (f32[6,4,64,128]{3,2,1,0:T(8,128)S(1)}, f32[6,4,64,128]{3,2,1,0:T(8,128)S(1)}) custom-call(f32[6,4,64,128]{3,2,1,0:T(8,128)} %bitcast.9, s32[2,64]{1,0:T(2,128)S(1)} %bitcast.7, f32[2,64]{1,0:T(2,128)S(1)} %bitcast.8, s32[1]{0:T(128)S(6)} %copy.8.count), custom_call_target="tpu_custom_call" | custom-call | flops 20000000 | bytes 2359296 | tf_op jit(solution)/shard_map/pallas_call | solution.py:585
  56.4 0.9 %copy.9 = f32[1,6,4,64,128]{4,3,2,1,0:T(8,128)} copy(f32[1,6,4,64,128]{4,3,2,1,0:T(8,128)S(1)} %bitcast.6) | data formatting | bytes 1572864
  57.3 0.9 %copy.10 = f32[1,6,4,64,128]{4,3,2,1,0:T(8,128)} copy(f32[1,6,4,64,128]{4,3,2,1,0:T(8,128)S(1)} %bitcast.5) | data formatting | bytes 1572864
Async XLA Ops:
  1.3 0.7 %copy-start.1 = (f32[1,2,64]{2,1,0:T(2,128)S(1)}, f32[1,2,64]{2,1,0:T(2,128)}, u32[]{:S(2)}) copy-start(f32[1,2,64]{2,1,0:T(2,128)} %param.6) | copy-start | bytes 1540
  1.3 0.7 %copy-start = (s32[1,2,64]{2,1,0:T(2,128)S(1)}, s32[1,2,64]{2,1,0:T(2,128)}, u32[]{:S(2)}) copy-start(s32[1,2,64]{2,1,0:T(2,128)} %param.5) | copy-start | bytes 1540

commit v11 on v9

--- a/solution.py
+++ b/solution.py
@@ -194,18 +194,25 @@
             return in_n.at[slot]
         return ww.at[spot, :, pl.ds(pl.multiple_of(at + 8, 8), SLAB)]
 
-    def send(unit, part):
-        target = target_of(unit, part, inst)
+    def send(unit, part, part_v):
+        some = pl.ds(NV // 2 * part_v, NV // 2)
+        target = target_of(unit, part, inst).at[some]
+        came = p_recv.at[unit, part, part_v]
         for j in others:
-            remote(
-                source_of(unit, j, part), target, p_send.at[unit], p_recv.at[unit, part], (j, dom)
-            ).start()
-        pltpu.make_async_copy(source_of(unit, inst, part), target, p_recv.at[unit, part]).start()
-
-    def arrive(unit, part):
+            source = source_of(unit, j, part).at[some]
+            remote(source, target, p_send.at[unit], came, (j, dom)).start()
+        pltpu.make_async_copy(source_of(unit, inst, part).at[some], target, came).start()
+
+    def arrive(unit, part, part_v):
         spots = pl.ds(2 * part, 2)
-        ref = (in_u.at[part], ss.at[spots], in_n, ww.at[spots, :, pl.ds(8, T)])[unit]
-        pltpu.make_async_copy(ref, ref, p_recv.at[unit, part]).wait()
+        some = pl.ds(NV // 2 * part_v, NV // 2)
+        ref = (
+            in_u.at[part, :, some],
+            ss.at[spots, some],
+            in_n.at[:, some],
+            ww.at[spots, some, pl.ds(8, T)],
+        )[unit]
+        pltpu.make_async_copy(ref, ref, p_recv.at[unit, part, part_v]).wait()
 
     def gone(unit):
         ref = in_n.at[0 : NI - 1] if unit == 2 else w1.at[:, 0 : NI - 1]
@@ -242,8 +249,9 @@
             out.append(6.0 * h + (after - prior))
         return out
 
-    def spectral(part, target, plus=None):
-        def variable(v):
+    def spectral(part, part_v, target, plus=None):
+        def variable(n):
+            v = NV // 2 * part_v + n
             for t0 in range(0, SLAB, 8):
                 rows = slice(t0, t0 + 8)
                 if plus is None:
@@ -253,7 +261,7 @@
                 for m, g in enumerate(spectral_apply(x)):
                     target[part, m, v, rows, :] = g
 
-        over(NV, variable)
+        over(NV // 2, variable)
 
     def inside(out, first_tile, last_tile):
         def tile(i, _):
@@ -352,7 +360,8 @@
 
     pl.semaphore_wait(barrier, NI + 3)
     for part in range(2):
-        send(0, part)
+        for k in range(2):
+            send(0, part, k)
     for c in loads:
         c.wait()
     active = jnp.where(lax.broadcasted_iota(jnp.int32, (1, S), 1) < count_s[0], 1.0, 0.0)
@@ -386,13 +395,15 @@
             coef[side, i] = jnp.broadcast_to(column, (T, S))
 
     half = T // 16
-    arrive(0, 0)
-    spectral(0, w1)
-    send(1, 0)
+    for k in range(2):
+        arrive(0, 0, k)
+        spectral(0, k, w1)
+        send(1, 0, k)
     inside(n0, 0, half)
-    arrive(0, 1)
-    spectral(1, w1)
-    send(1, 1)
+    for k in range(2):
+        arrive(0, 1, k)
+        spectral(1, k, w1)
+        send(1, 1, k)
     for v in range(NV):
         slab_out[0, v] = in_u[1, :, v, 0, :]
         slab_out[1, v] = in_u[1, :, v, SLAB - 1, :]
@@ -407,7 +418,8 @@
     for c in windows:
         c.wait_recv()
     interface(n0, 0, (0, T // 8, 1))
-    send(2, 0)
+    for k in range(2):
+        send(2, 0, k)
 
     toward = jnp.where(body == 0, 1.0, -1.0)
 
@@ -443,7 +455,8 @@
             slab_a[m, v, t0 + 1 : t0 + 9, :] - slab_b[m, v, t0 + 7 : t0 + 15, :]
         )
 
-    spectral(1, w2, outer)
+    for k in range(2):
+        spectral(1, k, w2, outer)
 
     def keep_rows(out, spots, times, value):
         for spot in spots:
@@ -483,11 +496,13 @@
     def first_sum(spot, t):
         return n0[:, ORDER[spot], t, :] + ss[spot, :, t, :]
 
-    arrive(1, 0)
+    arrive(1, 0, 0)
+    arrive(1, 0, 1)
     keep_rows(redge, (0, 1), ends, first_sum)
     rim = rim_of(4, redge, rhalo, FRONT)
     sums((0, 1))
-    arrive(1, 1)
+    arrive(1, 1, 0)
+    arrive(1, 1, 1)
     keep_rows(redge, (2, 3), ends, first_sum)
     rim2 = rim_of(6, redge, rhalo, REST)
     for c in rim:
@@ -498,7 +513,8 @@
         c.wait_send()
     first_update((0, 1))
     windows = interface_rows(1)
-    send(3, 1)
+    for k in range(2):
+        send(3, 1, k)
     sums((2, 3))
     for c in rim2:
         c.wait()
@@ -506,9 +522,10 @@
     first_update((2, 3))
     layers = outer_layers(1)
 
-    arrive(2, 0)
-    spectral(0, w2, lambda m, v, t0: in_n[m, v, t0 : t0 + 8, :])
-    send(3, 0)
+    for k in range(2):
+        arrive(2, 0, k)
+        spectral(0, k, w2, lambda m, v, t0: in_n[m, v, t0 : t0 + 8, :])
+        send(3, 0, k)
     inside(n1, 0, 2 * half)
     around(n1, 1, layers)
 
@@ -529,10 +546,12 @@
     def last_source(spot, t):
         return ww[spot, :, 8 + t, :]
 
-    arrive(3, 1)
+    arrive(3, 1, 0)
+    arrive(3, 1, 1)
     keep_rows(wedge, (2, 3), far_rows, last_source)
     far2 = rim_of(16, wedge, whalo, REST)
-    arrive(3, 0)
+    arrive(3, 0, 0)
+    arrive(3, 0, 1)
     keep_rows(wedge, (0, 1), far_rows, last_source)
     far = rim_of(20, wedge, whalo, FRONT)
 
@@ -624,7 +643,7 @@
             pltpu.VMEM((2, NV, NI, S), f32),
             pltpu.SemaphoreType.DMA((5,)),
             pltpu.SemaphoreType.DMA((4,)),
-            pltpu.SemaphoreType.DMA((4, 2)),
+            pltpu.SemaphoreType.DMA((4, 2, 2)),
             pltpu.SemaphoreType.DMA((22,)),
             pltpu.SemaphoreType.DMA((22,)),
         ],

time: 57.5 us -> 58.4 us (1.016); the launches traced: 57.3 us -> 57.4 us
  no operation moved by 1% of the time
where the time goes in v11:
time: 58.4 us; the launch traced here: 57.4 us
  Pallas kernels  53.6 us (92%)
  local copies, waits for them, and re-layouts  2.44 us (4%)
  between operations  1.3 us (2%)
    pallas_call x1, Pallas kernels, local(): pl.pallas_call(functools.partial(kernel, n_dom, n_dom * T), out_shape=[ja...  53.6 us
    unnamed x6, local copies, waits for them, and re-layouts  2.44 us

profile of v11, /device:TPU:0, one launch (start us, length us, event | category | flops | bytes accessed | tf_op | source)
XLA Modules:
  0.0 57.4 jit_solution(17128164267434222807)
XLA Ops:
  1.3 0.0 copy-start.1
  1.3 0.0 copy-start
  1.3 0.7 %copy-done.1 = f32[1,2,64]{2,1,0:T(2,128)S(1)} copy-done((f32[1,2,64]{2,1,0:T(2,128)S(1)}, f32[1,2,64]{2,1,0:T(2,128)}, u32[]{:S(2)}) %copy-start.1) | copy-done | bytes 536
  2.0 0.0 copy-done
  2.0 53.6 %shard_map.59 = (f32[6,4,64,128]{3,2,1,0:T(8,128)S(1)}, f32[6,4,64,128]{3,2,1,0:T(8,128)S(1)}) custom-call(f32[6,4,64,128]{3,2,1,0:T(8,128)} %bitcast.9, s32[2,64]{1,0:T(2,128)S(1)} %bitcast.7, f32[2,64]{1,0:T(2,128)S(1)} %bitcast.8, s32[1]{0:T(128)S(6)} %copy.8.count), custom_call_target="tpu_custom_call" | custom-call | flops 20000000 | bytes 2359296 | tf_op jit(solution)/shard_map/pallas_call | solution.py:607
  55.6 0.9 %copy.9 = f32[1,6,4,64,128]{4,3,2,1,0:T(8,128)} copy(f32[1,6,4,64,128]{4,3,2,1,0:T(8,128)S(1)} %bitcast.6) | data formatting | bytes 1572864
  56.5 0.9 %copy.10 = f32[1,6,4,64,128]{4,3,2,1,0:T(8,128)} copy(f32[1,6,4,64,128]{4,3,2,1,0:T(8,128)S(1)} %bitcast.5) | data formatting | bytes 1572864
Async XLA Ops:
  1.3 0.7 %copy-start.1 = (f32[1,2,64]{2,1,0:T(2,128)S(1)}, f32[1,2,64]{2,1,0:T(2,128)}, u32[]{:S(2)}) copy-start(f32[1,2,64]{2,1,0:T(2,128)} %param.6) | copy-start | bytes 1540
  1.3 0.7 %copy-start = (s32[1,2,64]{2,1,0:T(2,128)S(1)}, s32[1,2,64]{2,1,0:T(2,128)}, u32[]{:S(2)}) copy-start(s32[1,2,64]{2,1,0:T(2,128)} %param.5) | copy-start | bytes 1540

commit v12 on v9

--- a/solution.py
+++ b/solution.py
@@ -506,10 +506,11 @@
     first_update((2, 3))
     layers = outer_layers(1)
 
+    inside(n1, 0, half)
     arrive(2, 0)
     spectral(0, w2, lambda m, v, t0: in_n[m, v, t0 : t0 + 8, :])
     send(3, 0)
-    inside(n1, 0, 2 * half)
+    inside(n1, half, 2 * half)
     around(n1, 1, layers)
 
     def second_sum(spot, t):

time: 57.5 us -> 57.5 us (level)
  no operation moved by 1% of the time
where the time goes in v12:
time: 57.5 us; the launch traced here: 57.3 us
  Pallas kernels  53.6 us (93%)
  local copies, waits for them, and re-layouts  2.44 us (4%)
  between operations  1.3 us (2%)
    pallas_call x1, Pallas kernels, local(): pl.pallas_call(functools.partial(kernel, n_dom, n_dom * T), out_shape=[ja...  53.6 us
    unnamed x6, local copies, waits for them, and re-layouts  2.44 us

profile of v12, /device:TPU:0, one launch (start us, length us, event | category | flops | bytes accessed | tf_op | source)
XLA Modules:
  0.0 57.3 jit_solution(12298821359681957665)
XLA Ops:
  1.3 0.0 copy-start.1
  1.3 0.0 copy-start
  1.3 0.7 %copy-done.1 = f32[1,2,64]{2,1,0:T(2,128)S(1)} copy-done((f32[1,2,64]{2,1,0:T(2,128)S(1)}, f32[1,2,64]{2,1,0:T(2,128)}, u32[]{:S(2)}) %copy-start.1) | copy-done | bytes 536
  2.0 0.0 copy-done
  2.0 53.6 %shard_map.59 = (f32[6,4,64,128]{3,2,1,0:T(8,128)S(1)}, f32[6,4,64,128]{3,2,1,0:T(8,128)S(1)}) custom-call(f32[6,4,64,128]{3,2,1,0:T(8,128)} %bitcast.9, s32[2,64]{1,0:T(2,128)S(1)} %bitcast.7, f32[2,64]{1,0:T(2,128)S(1)} %bitcast.8, s32[1]{0:T(128)S(6)} %copy.8.count), custom_call_target="tpu_custom_call" | custom-call | flops 20000000 | bytes 2359296 | tf_op jit(solution)/shard_map/pallas_call | solution.py:589
  55.5 0.9 %copy.9 = f32[1,6,4,64,128]{4,3,2,1,0:T(8,128)} copy(f32[1,6,4,64,128]{4,3,2,1,0:T(8,128)S(1)} %bitcast.6) | data formatting | bytes 1572864
  56.4 0.9 %copy.10 = f32[1,6,4,64,128]{4,3,2,1,0:T(8,128)} copy(f32[1,6,4,64,128]{4,3,2,1,0:T(8,128)S(1)} %bitcast.5) | data formatting | bytes 1572864
Async XLA Ops:
  1.3 0.7 %copy-start.1 = (f32[1,2,64]{2,1,0:T(2,128)S(1)}, f32[1,2,64]{2,1,0:T(2,128)}, u32[]{:S(2)}) copy-start(f32[1,2,64]{2,1,0:T(2,128)} %param.6) | copy-start | bytes 1540
  1.3 0.7 %copy-start = (s32[1,2,64]{2,1,0:T(2,128)S(1)}, s32[1,2,64]{2,1,0:T(2,128)}, u32[]{:S(2)}) copy-start(s32[1,2,64]{2,1,0:T(2,128)} %param.5) | copy-start | bytes 1540

commit v13 on v10

--- a/solution.py
+++ b/solution.py
@@ -140,13 +140,8 @@
     left = lax.rem(dom + n_dom - 1, n_dom)
     right = lax.rem(dom + 1, n_dom)
 
+    others = [lax.rem(inst + n, NI) for n in range(1, NI)]
     body, place = inst // ZN, lax.rem(inst, ZN)
-    others = [
-        lax.rem(body + other, 2) * ZN + lax.rem(place + dz, ZN)
-        for other in (1, 0)
-        for dz in (2, 1, 3, 0)
-        if other or dz
-    ]
     at_start = jnp.where(place == 0, 1, 0)
     at_end = jnp.where(place == ZN - 1, 1, 0)
     before = lax.rem(dom + n_dom - at_start, n_dom)
@@ -509,10 +504,11 @@
     first_update((2, 3))
     layers = outer_layers(1)
 
+    inside(n1, 0, half)
     arrive(2, 0)
     spectral(0, w2, lambda m, v, t0: in_n[m, v, t0 : t0 + 8, :])
     send(3, 0)
-    inside(n1, 0, 2 * half)
+    inside(n1, half, 2 * half)
     around(n1, 1, layers)
 
     def second_sum(spot, v, t0, t1):

time: 58.3 us -> 57.5 us (0.986)
  Pallas kernels: 54.4 us -> 53.6 us
    pallas_call x1, Pallas kernels: 54.4 us -> 53.6 us  [local(): pl.pallas_call(functools.partial(kernel, n_dom, n_dom * T), out_shape=[ja...]
where the time goes in v13:
time: 57.5 us; the launch traced here: 57.3 us
  Pallas kernels  53.6 us (93%)
  local copies, waits for them, and re-layouts  2.44 us (4%)
  between operations  1.3 us (2%)
    pallas_call x1, Pallas kernels, local(): pl.pallas_call(functools.partial(kernel, n_dom, n_dom * T), out_shape=[ja...  53.6 us
    unnamed x6, local copies, waits for them, and re-layouts  2.44 us

profile of v13, /device:TPU:0, one launch (start us, length us, event | category | flops | bytes accessed | tf_op | source)
XLA Modules:
  0.0 57.3 jit_solution(11968046201793098566)
XLA Ops:
  1.3 0.0 copy-start.1
  1.3 0.0 copy-start
  1.3 0.7 %copy-done.1 = f32[1,2,64]{2,1,0:T(2,128)S(1)} copy-done((f32[1,2,64]{2,1,0:T(2,128)S(1)}, f32[1,2,64]{2,1,0:T(2,128)}, u32[]{:S(2)}) %copy-start.1) | copy-done | bytes 536
  2.0 0.0 copy-done
  2.0 53.6 %shard_map.59 = (f32[6,4,64,128]{3,2,1,0:T(8,128)S(1)}, f32[6,4,64,128]{3,2,1,0:T(8,128)S(1)}) custom-call(f32[6,4,64,128]{3,2,1,0:T(8,128)} %bitcast.9, s32[2,64]{1,0:T(2,128)S(1)} %bitcast.7, f32[2,64]{1,0:T(2,128)S(1)} %bitcast.8, s32[1]{0:T(128)S(6)} %copy.8.count), custom_call_target="tpu_custom_call" | custom-call | flops 20000000 | bytes 2359296 | tf_op jit(solution)/shard_map/pallas_call | solution.py:581
  55.6 0.9 %copy.9 = f32[1,6,4,64,128]{4,3,2,1,0:T(8,128)} copy(f32[1,6,4,64,128]{4,3,2,1,0:T(8,128)S(1)} %bitcast.6) | data formatting | bytes 1572864
  56.5 0.9 %copy.10 = f32[1,6,4,64,128]{4,3,2,1,0:T(8,128)} copy(f32[1,6,4,64,128]{4,3,2,1,0:T(8,128)S(1)} %bitcast.5) | data formatting | bytes 1572864
Async XLA Ops:
  1.3 0.7 %copy-start.1 = (f32[1,2,64]{2,1,0:T(2,128)S(1)}, f32[1,2,64]{2,1,0:T(2,128)}, u32[]{:S(2)}) copy-start(f32[1,2,64]{2,1,0:T(2,128)} %param.6) | copy-start | bytes 1540
  1.3 0.7 %copy-start = (s32[1,2,64]{2,1,0:T(2,128)S(1)}, s32[1,2,64]{2,1,0:T(2,128)}, u32[]{:S(2)}) copy-start(s32[1,2,64]{2,1,0:T(2,128)} %param.5) | copy-start | bytes 1540
